TPU v7x, 32 devices: a whole 2x2x4 slice. The times are simulated.
32 devices in a mesh: arrow: 4 (over x, core), blk: 8 (over z, y).
Axes of the slice: x: 2, y: 2, z: 4, core: 2. Of those that a mesh axis runs over, the one named last changes fastest.
Arguments:
- features: bfloat16 [8192, 512], P(('arrow', 'blk')), may hold values from -6 to 6
- positions: int32 [4, 8192], P(None, ('arrow', 'blk')), may hold values from 0 to 8191, as said below
- diag_values: bfloat16 [4096, 8192], P('arrow', 'blk'), may hold values from -0.1875 to 0.1875
- column_values: bfloat16 [4096, 8192], P('arrow', 'blk'), may hold values from -0.1875 to 0.1875
- row_values: bfloat16 [4096, 8192], P('arrow', 'blk'), may hold values from -0.0625 to 0.0625
- tile_masks: int32 [3, 32, 64], P(None, 'arrow', 'blk'), may hold values from 0 to 1, as said below
- up_weight: bfloat16 [1024, 4096], replicated, may hold values from -0.1875 to 0.1875
- down_weight: bfloat16 [4096, 512], replicated, may hold values from -0.09375 to 0.09375
Outputs:
- node_out: bfloat16 [8192, 512], P(('arrow', 'blk'))
Inputs may be any that keep to these rules, and one draw needn't show every extreme that they name: For each arrow, positions is a permutation of the nodes. The 256 nodes of one device put at most 48 nodes into any one block of 1024 positions of one arrow, and exactly 48 into some block. `tile_masks`: 1 marks a stored tile, 0 an empty one.
All inputs are finite; a program needn't handle non-finite values.
Results may differ from a plain program's by a relative error of at most 0.0085.
Values may be sent and summed in bfloat16 or wider, within the bound.
A program may use at most 64 MiB of HBM per device.

v0:
```python
import jax
import jax.numpy as jnp
from jax import lax
from jax.sharding import PartitionSpec as P


def spread(block, axis, source):
    block = jnp.where(lax.axis_index(axis) == source, block, jnp.zeros_like(block))
    return lax.psum(block, axis)


def masked_block(values, tiles):
    tile_count = tiles.shape[0]
    tile_edge = values.shape[0] // tile_count
    shaped = values.reshape(tile_count, tile_edge, tile_count, tile_edge)
    keep_mask = tiles.astype(values.dtype)[:, None, :, None]
    return (shaped * keep_mask).reshape(values.shape)


def body(
    features, positions, diag_values, column_values, row_values, tile_masks, up_weight, down_weight
):
    row_count = features.shape[0]
    feat_width = features.shape[1]
    arrow_count = positions.shape[0]
    block_count = lax.axis_size("blk")
    device_count = arrow_count * block_count
    block_rows = diag_values.shape[0]
    capacity = row_count // block_count + max(row_count // (2 * block_count), 1)
    flat_pos = positions.reshape(-1)
    arrow_ids = jnp.repeat(jnp.arange(arrow_count, dtype=jnp.int32), row_count)
    target_dev = arrow_ids * block_count + flat_pos // block_rows
    within_pos = flat_pos % block_rows
    onehot_dest = (
        target_dev[:, None] == jnp.arange(device_count, dtype=jnp.int32)[None, :]
    ).astype(jnp.int32)
    slot_rank = jnp.sum((jnp.cumsum(onehot_dest, axis=0) - 1) * onehot_dest, axis=1)
    slot_index = target_dev * capacity + slot_rank
    source_rows = jnp.tile(features, (arrow_count, 1))
    send_rows = (
        jnp.zeros((device_count * capacity, feat_width), features.dtype)
        .at[slot_index]
        .set(source_rows)
    )
    send_pos = (
        jnp.full((device_count * capacity,), block_rows, jnp.int32).at[slot_index].set(within_pos)
    )
    recv_rows, recv_pos = (
        lax.all_to_all(
            send_rows.reshape(device_count, capacity, feat_width),
            ("arrow", "blk"),
            split_axis=0,
            concat_axis=0,
            tiled=True,
        ),
        lax.all_to_all(
            send_pos.reshape(device_count, capacity),
            ("arrow", "blk"),
            split_axis=0,
            concat_axis=0,
            tiled=True,
        ),
    )
    recv_flat = recv_pos.reshape(-1)
    block_feats = (
        jnp.zeros((block_rows, feat_width), features.dtype)
        .at[recv_flat]
        .set(recv_rows.reshape(-1, feat_width), mode="drop")
    )
    head_block = spread(block_feats, "blk", 0)
    diag_full = masked_block(diag_values, tile_masks[0])
    column_full = masked_block(column_values, tile_masks[1])
    row_full = masked_block(row_values, tile_masks[2])
    arm_term = jnp.dot(row_full, block_feats, preferred_element_type=jnp.float32)
    local_sum = jnp.dot(diag_full, block_feats, preferred_element_type=jnp.float32)
    local_sum = local_sum + jnp.dot(column_full, head_block, preferred_element_type=jnp.float32)
    is_head = lax.axis_index("blk") == 0
    arm_total = lax.psum(arm_term.astype(jnp.bfloat16), "blk").astype(jnp.float32)
    results = jnp.where(is_head, local_sum + arm_total, local_sum).astype(jnp.bfloat16)
    picked = results[jnp.minimum(recv_flat, block_rows - 1)]
    returned = lax.all_to_all(
        picked.reshape(device_count, capacity, feat_width),
        ("arrow", "blk"),
        split_axis=0,
        concat_axis=0,
        tiled=True,
    )
    mine = returned.reshape(device_count * capacity, feat_width)[slot_index].reshape(
        arrow_count, row_count, feat_width
    )
    aggregate = jnp.sum(mine.astype(jnp.float32), axis=0).astype(jnp.bfloat16)
    joined = jnp.concatenate([features, aggregate], axis=1)
    hidden = jax.nn.silu(jnp.dot(joined, up_weight, preferred_element_type=jnp.float32)).astype(
        jnp.bfloat16
    )
    return jnp.dot(hidden, down_weight, preferred_element_type=jnp.float32).astype(jnp.bfloat16)


def solution(mesh):
    in_specs = (
        P(("arrow", "blk"), None),
        P(None, ("arrow", "blk")),
        P("arrow", "blk"),
        P("arrow", "blk"),
        P("arrow", "blk"),
        P(None, "arrow", "blk"),
        P(),
        P(),
    )
    out_specs = P(("arrow", "blk"), None)
    return jax.shard_map(body, mesh=mesh, in_specs=in_specs, out_specs=out_specs, check_vma=False)
```

profile of v0, /device:TPU:21, one launch (start us, length us, event | category | flops | bytes accessed | tf_op | source)
XLA Modules:
  0.0 264.0 jit_solution(8578962534028955260)
XLA Ops:
  6.6 0.7 reshape.255
  7.3 9.0 %reduce-window.6 = s32[32,8,128]{2,1,0:T(8,128)S(1)} reduce-window(s32[32,8,128]{2,1,0:T(8,128)S(1)} %fusion.26, s32[]{:T(128)} %constant.46.clone.1), window={size=1x1x128 pad=0_0x0_0x127_0}, to_apply=%region_0.1 | reduce-window | flops 4161536 | bytes 262148 | tf_op jit(solution)/shard_map/reduce-window
  16.3 0.1 slice.28
  16.4 0.1 copy.9
  16.6 0.1 copy.10
  16.6 0.1 add_add_fusion
  16.8 0.7 copy.15
  17.5 0.7 copy.13
  18.3 4.3 %scatter_custom_fusion = s32[1536]{0:T(1024)S(1)} fusion(s32[1024]{0:T(1024)S(1)} %bitcast.78, s32[1024]{0:T(1024)S(1)} %get-tuple-element.12, s32[]{:T(128)} %constant.48.clone.1), kind=kCustom, calls=%fused_computation.61 | custom fusion | bytes 6148 | tf_op jit(solution)/shard_map/scatter | solution.py:46
  22.6 0.7 all_to_all.12
  23.3 6.2 %all-to-all-start = ((s32[32,1,48]{2,1,0:T(1,128)}), s32[32,1,48]{2,1,0:T(1,128)S(1)}, u32[]{:S(2)}, u32[]{:S(2)}) async-start(s32[32,1,48]{2,1,0:T(1,128)} %all_to_all.12), calls=%async_computation | async-start | bytes 32768 | tf_op jit(solution)/shard_map/all_to_all | solution.py:56
  29.5 1.0 tile.4
  30.5 0.0 copy-start.1
  30.5 6.4 %scatter_custom_fusion.1 = bf16[1536,512]{1,0:T(8,128)(2,1)} fusion(s32[1024]{0:T(1024)S(1)} %bitcast.79, bf16[1024,512]{1,0:T(8,128)(2,1)S(1)} %bitcast.72, bf16[]{:T(256)} %constant.47.clone.1), kind=kCustom, calls=%fused_computation.21 | custom fusion | bytes 1572866 | tf_op jit(solution)/shard_map/scatter | solution.py:43
  36.9 0.0 all-to-all-done
  36.9 5.8 %all-to-all-start.1 = ((bf16[32,48,512]{2,1,0:T(8,128)(2,1)}), bf16[32,48,512]{2,1,0:T(8,128)(2,1)S(1)}, u32[]{:S(2)}, u32[]{:S(2)}) async-start(bf16[32,48,512]{2,1,0:T(8,128)(2,1)} %bitcast.6), calls=%async_computation.1 | async-start | bytes 3145728 | tf_op jit(solution)/shard_map/all_to_all | solution.py:49
  42.8 0.0 all-reduce.3.cloned.1.call-start
  42.8 0.0 copy-done.1
  42.9 0.5 broadcast.253
  43.4 0.7 reduce.8
  44.1 0.1 reshape.257
  44.2 33.8 %all-to-all-done.1 = bf16[32,48,512]{2,1,0:T(8,128)(2,1)S(1)} async-done(((bf16[32,48,512]{2,1,0:T(8,128)(2,1)}), bf16[32,48,512]{2,1,0:T(8,128)(2,1)S(1)}, u32[]{:S(2)}, u32[]{:S(2)}) %all-to-all-start.1) | async-done | bytes 1572896 | tf_op jit(solution)/shard_map/all_to_all | solution.py:49
  78.0 7.7 %scatter_custom_fusion.2 = bf16[1024,512]{1,0:T(8,128)(2,1)S(1)} fusion(s32[1536]{0:T(1024)S(1)} %get-tuple-element.6, bf16[1536,512]{1,0:T(8,128)(2,1)S(1)} %bitcast.71, bf16[]{:T(256)} %constant.47.clone.1), kind=kCustom, calls=%fused_computation.27 | custom fusion | bytes 1048578 | tf_op jit(solution)/shard_map/scatter | solution.py:68
  85.7 0.0 copy-start.2
  85.7 1.1 broadcast_select_fusion
  86.8 0.3 mul.97
  87.1 0.6 copy-done.2
  87.7 2.2 fusion.8
  89.9 0.0 copy-start.3
  89.9 0.0 all-reduce.3.cloned.1.call-update
  89.9 102.8 %all-reduce.3.cloned.1.call-done = (bf16[1024,512]{1,0:T(8,128)(2,1)}, bf16[1024,512]{1,0:T(8,128)(2,1)}) async-done(((bf16[1024,512]{1,0:T(8,128)(2,1)}, bf16[1024,512]{1,0:T(8,128)(2,1)}), (bf16[1024,512]{1,0:T(8,128)(2,1)}, bf16[1024,512]{1,0:T(8,128)(2,1)})) %all-reduce.3.cloned.1.call-update) | async-done | bytes 2097168 | tf_op jit(solution)/shard_map/psum | solution.py:78
  192.8 0.3 mul.94
  193.1 0.0 copy-done.3
  193.1 0.9 copy-done.6
  194.0 0.0 copy-start.5
  194.0 1.2 fusion.3
  195.2 0.0 copy-start.4
  195.2 0.3 mul.83
  195.6 0.0 copy-done.5
  195.6 1.2 copy-done.4
  196.8 1.3 fusion
  198.2 5.4 %gather_fusion = bf16[1536,512]{1,0:T(8,128)(2,1)} fusion(bf16[1024,512]{1,0:T(8,128)(2,1)S(1)} %fusion, s32[2048]{0:T(1024)S(1)} %pad_clamp_fusion), kind=kCustom, calls=%fused_computation | custom fusion | bytes 3151872 | tf_op jit(solution)/shard_map/gather | solution.py:80
  203.6 5.2 %all-to-all-start.2 = ((bf16[32,48,512]{2,1,0:T(8,128)(2,1)}), bf16[32,48,512]{2,1,0:T(8,128)(2,1)S(1)}, u32[]{:S(2)}, u32[]{:S(2)}) async-start(bf16[32,48,512]{2,1,0:T(8,128)(2,1)} %bitcast.10), calls=%async_computation.2 | async-start | bytes 3145728 | tf_op jit(solution)/shard_map/all_to_all | solution.py:81
  208.8 35.2 %all-to-all-done.2 = bf16[32,48,512]{2,1,0:T(8,128)(2,1)S(1)} async-done(((bf16[32,48,512]{2,1,0:T(8,128)(2,1)}), bf16[32,48,512]{2,1,0:T(8,128)(2,1)S(1)}, u32[]{:S(2)}, u32[]{:S(2)}) %all-to-all-start.2) | async-done | bytes 1572896 | tf_op jit(solution)/shard_map/all_to_all | solution.py:81
  244.0 4.0 %gather_fusion.1 = bf16[1024,512]{1,0:T(8,128)(2,1)S(1)} fusion(bf16[1536,512]{1,0:T(8,128)(2,1)S(1)} %bitcast.66, s32[1024]{0:T(1024)S(1)} %broadcast_clamp_fusion), kind=kCustom, calls=%fused_computation.1 | custom fusion | bytes 2101248 | tf_op jit(solution)/shard_map/gather | solution.py:88
  247.9 0.2 reduce_sum.25
  248.2 0.0 copy-done
  248.2 9.0 %fusion.9 = bf16[256,512]{1,0:T(8,128)(2,1)} fusion(bf16[4096,512]{1,0:T(8,128)(2,1)} %param.15, bf16[1024,4096]{1,0:T(8,128)(2,1)} %param.14, bf16[256,512]{1,0:T(8,128)(2,1)S(1)} %reduce_sum.25, bf16[256,512]{1,0:T(8,128)(2,1)S(1)} %copy-done), kind=kOutput, calls=%fused_computation.19 | convolution fusion | flops 3227648000 | bytes 13369344 | tf_op jit(solution)/shard_map/dot_general | solution.py:96
  (20 shorter events, 0.2 us)
Async XLA Ops:
  23.3 13.7 %all-to-all-start = ((s32[32,1,48]{2,1,0:T(1,128)}), s32[32,1,48]{2,1,0:T(1,128)S(1)}, u32[]{:S(2)}, u32[]{:S(2)}) async-start(s32[32,1,48]{2,1,0:T(1,128)} %all_to_all.12), calls=%async_computation | async-start | bytes 32768 | tf_op jit(solution)/shard_map/all_to_all | solution.py:56
  30.5 12.3 %copy-start.1 = (s32[3,8,8]{2,1,0:T(8,128)S(1)}, s32[3,8,8]{2,1,0:T(8,128)}, u32[]{:S(2)}) copy-start(s32[3,8,8]{2,1,0:T(8,128)} %param.13) | copy-start | bytes 2308
  36.9 41.0 %all-to-all-start.1 = ((bf16[32,48,512]{2,1,0:T(8,128)(2,1)}), bf16[32,48,512]{2,1,0:T(8,128)(2,1)S(1)}, u32[]{:S(2)}, u32[]{:S(2)}) async-start(bf16[32,48,512]{2,1,0:T(8,128)(2,1)} %bitcast.6), calls=%async_computation.1 | async-start | bytes 3145728 | tf_op jit(solution)/shard_map/all_to_all | solution.py:49
  42.8 150.0 %all-reduce.3.cloned.1.call-start = ((), (), s32[]{:S(2)}) async-start(), calls=%async_computation.3 | async-start | bytes 4194304 | tf_op jit(solution)/shard_map/psum | solution.py:78
  85.7 2.0 copy-start.2
  89.9 103.2 %copy-start.3 = (bf16[1024,1024]{1,0:T(8,128)(2,1)S(1)}, bf16[1024,1024]{1,0:T(8,128)(2,1)}, u32[]{:S(2)}) copy-start(bf16[1024,1024]{1,0:T(8,128)(2,1)} %param.11) | copy-start | bytes 6291460
  192.8 1.2 copy-start.6
  194.0 1.6 copy-start.5
  195.2 1.6 copy-start.4
  203.6 40.4 %all-to-all-start.2 = ((bf16[32,48,512]{2,1,0:T(8,128)(2,1)}), bf16[32,48,512]{2,1,0:T(8,128)(2,1)S(1)}, u32[]{:S(2)}, u32[]{:S(2)}) async-start(bf16[32,48,512]{2,1,0:T(8,128)(2,1)} %bitcast.10), calls=%async_computation.2 | async-start | bytes 3145728 | tf_op jit(solution)/shard_map/all_to_all | solution.py:81
  244.0 4.2 %copy-start = (bf16[256,512]{1,0:T(8,128)(2,1)S(1)}, bf16[256,512]{1,0:T(8,128)(2,1)}, u32[]{:S(2)}) copy-start(bf16[256,512]{1,0:T(8,128)(2,1)} %param.8) | copy-start | bytes 786436
Sparse Core Ops, SparseCore 0:
  90.0 102.6 all-reduce.2
where the time goes:
time: 269 us; the launch traced here: 264 us
  waiting for transfers between devices  172 us (64%)
  local copies, waits for them, and re-layouts  36.2 us (13%)
  starting transfers between devices  17.2 us (6%)
  matrix products  13.8 us (5%)
  between operations  13.7 us (5%)
  other arithmetic  11.3 us (4%)
    psum x1, waiting for transfers between devices, body(): lax.psum(arm_term.astype(jnp.bfloat16), 'blk').astype(jnp.float32)  103 us
    all_to_all x1, waiting for transfers between devices, body(): lax.all_to_all(picked.reshape(device_count, capacity, feat_width), ('arro...  35.2 us
    all_to_all x1, waiting for transfers between devices, body(): lax.all_to_all(send_rows.reshape(device_count, capacity, feat_width), ('a...  33.8 us
    another operation x3, other arithmetic  9.05 us
    dot_general x1, matrix products, body(): jnp.dot(hidden, down_weight, preferred_element_type=jnp.float32)  8.96 us
    scatter x1, local copies, waits for them, and re-layouts, body(): block_feats = jnp.zeros((block_rows, feat_width), features.dtype).at[recv...  7.72 us
    scatter x1, local copies, waits for them, and re-layouts, body(): send_rows = jnp.zeros((device_count * capacity, feat_width), features.dty...  6.39 us
    all_to_all x1, starting transfers between devices, body(): lax.all_to_all(send_pos.reshape(device_count, capacity), ('arrow', 'blk')...  6.2 us
  transfers between devices with their start and end apart: 4, of which 3 were waited for; matrix products, arithmetic and copies ran while one was open for 3% of the time, Pallas kernels for 0%

commit v1 on v0

v1 whole, which is shorter than its diff:
```python
import functools

import jax
import jax.numpy as jnp
from jax import lax
from jax.experimental import pallas as pl
from jax.experimental.pallas import tpu as pltpu
from jax.sharding import PartitionSpec as P

MESH = pl.DeviceIdType.MESH


def gather_kernel(dims, shard_ref, x_ref, xh_ref, st_ref, held, pos, rank, packed, sth,
                  zs, zr, xs, xr, ys, yr, dxs, dxr, dys, dyr, cs, cr, own_sem):
    nb, rows, cap, block_rows = dims
    lines = nb // 2
    n_dev = 4 * nb
    padded, width = shard_ref.shape
    half = (padded // 2 + 15) // 16 * 16
    a, b = lax.axis_index("arrow"), lax.axis_index("blk")
    ao, c, bo, bi = a // 2, a % 2, b // 2, b % 2
    up, down = (a, b + 2), (a, b - 2)
    across = ((1 - ao) * 2 + c, b)
    beside = (a, bo * 2 + 1 - bi)
    core = (ao * 2 + 1 - c, b)

    def column(ao_, c_, bi_):
        return (ao_ * 2 + c_) * 2 + bi_

    mine = column(ao, c, bi)
    x_col = column(1 - ao, c, bi)
    y_col = column(ao, c, 1 - bi)
    d_col = column(1 - ao, c, 1 - bi)
    cols = (mine, x_col, y_col, d_col)
    other = (column(ao, 1 - c, bi), column(1 - ao, 1 - c, bi), column(ao, 1 - c, 1 - bi),
             column(1 - ao, 1 - c, 1 - bi))
    whole_rows = pl.ds(0, padded)
    top, low = pl.ds(0, half), pl.ds(half, padded - half)

    def send(col, k, part, ssem, rsem, device):
        view = held.at[col, k, part]
        return pltpu.make_async_remote_copy(
            src_ref=view, dst_ref=view, send_sem=ssem, recv_sem=rsem,
            device_id=device, device_id_type=MESH)

    def z_up(k):
        return send(mine, k, whole_rows, zs.at[0, k], zr.at[k], up)

    def z_down(k):
        return send(mine, k, whole_rows, zs.at[1, k], zr.at[k], down)

    def x_send(k):
        return send(mine, k, whole_rows, xs.at[k], xr.at[k], across)

    def y_send(k):
        return send(mine, k, whole_rows, ys.at[k], yr.at[k], beside)

    def dy_send(k):
        return send(x_col, k, top, dys.at[k], dyr.at[k], beside)

    def dx_send(k):
        return send(y_col, k, low, dxs.at[k], dxr.at[k], across)

    def core_send(kind, k):
        return send(cols[kind], k, whole_rows, cs.at[kind, k], cr.at[kind, k], core)

    own = pltpu.make_async_copy(shard_ref, held.at[mine, bo], own_sem)
    own.start()
    barrier = pltpu.get_barrier_semaphore()
    for device in (across, beside, core):
        pl.semaphore_signal(barrier, inc=1, device_id=device, device_id_type=MESH)

    @pl.when(bo < lines - 1)
    def _():
        pl.semaphore_signal(barrier, inc=1, device_id=up, device_id_type=MESH)

    @pl.when(bo > 0)
    def _():
        pl.semaphore_signal(barrier, inc=1, device_id=down, device_id_type=MESH)

    ends = (bo < lines - 1).astype(jnp.int32) + (bo > 0).astype(jnp.int32)
    pl.semaphore_wait(barrier, 3 + ends)

    own.wait()

    def step(t, carry):
        for sign in (-1, 1):
            k = bo + sign * t
            ok = (k >= 0) & (k < lines) & (t < lines)
            if sign == 1:
                ok = ok & (t > 0)

            @pl.when(ok)
            def _():
                @pl.when(t > 0)
                def _():
                    send(mine, k, whole_rows, zs.at[0, k], zr.at[k], up).wait_recv()

                @pl.when((k <= bo) & (bo < lines - 1))
                def _():
                    z_up(k).start()

                @pl.when((k >= bo) & (bo > 0))
                def _():
                    z_down(k).start()

                x_send(k).start()
                y_send(k).start()
                core_send(0, k).start()

        for sign in (-1, 1):
            t2 = t - 1
            k2 = bo + sign * t2
            ok2 = (k2 >= 0) & (k2 < lines) & (t2 >= 0) & (t2 < lines)
            if sign == 1:
                ok2 = ok2 & (t2 > 0)

            @pl.when(ok2)
            def _():
                send(x_col, k2, whole_rows, xs.at[k2], xr.at[k2], across).wait_recv()
                dy_send(k2).start()
                core_send(1, k2).start()
                send(y_col, k2, whole_rows, ys.at[k2], yr.at[k2], beside).wait_recv()
                dx_send(k2).start()
                core_send(2, k2).start()

        for sign in (-1, 1):
            t3 = t - 2
            k3 = bo + sign * t3
            ok3 = (k3 >= 0) & (k3 < lines) & (t3 >= 0)
            if sign == 1:
                ok3 = ok3 & (t3 > 0)

            @pl.when(ok3)
            def _():
                send(d_col, k3, top, dys.at[k3], dyr.at[k3], beside).wait_recv()
                send(d_col, k3, low, dxs.at[k3], dxr.at[k3], across).wait_recv()
                core_send(3, k3).start()

        return carry

    lax.fori_loop(0, lines + 2, step, 0)

    def arrive(k, carry):
        for kind in range(4):
            send(other[kind], k, whole_rows, cs.at[kind, k], cr.at[kind, k], core).wait_recv()
        return carry

    lax.fori_loop(0, lines, arrive, 0)

    extra = padded - rows
    row_id = lax.broadcasted_iota(jnp.int32, (extra, rows), 0)
    weight = jnp.where(row_id == 2 * a, 256.0, jnp.where(row_id == 2 * a + 1, 1.0, 0.0))

    def read_pos(s, carry):
        sa, sb = s // nb, s % nb
        digits = held[sa * 2 + sb % 2, sb // 2, pl.ds(rows, extra), pl.ds(0, rows)]
        pos[pl.ds(s, 1), :] = jnp.sum(digits.astype(jnp.float32) * weight, axis=0, keepdims=True)
        return carry

    lax.fori_loop(0, n_dev, read_pos, 0)
    every = pos[...].astype(jnp.int32)
    before = (lax.broadcasted_iota(jnp.int32, (rows, rows), 0)
              < lax.broadcasted_iota(jnp.int32, (rows, rows), 1)).astype(jnp.float32).astype(jnp.bfloat16)
    for kind, block in ((0, b), (1, 0)):
        inside = (every >= block * block_rows) & (every < (block + 1) * block_rows)
        count = jnp.dot(inside.astype(jnp.float32).astype(jnp.bfloat16), before,
                        preferred_element_type=jnp.float32)
        rank[kind] = jnp.where(inside, count, -1.0)

    slot_id = lax.broadcasted_iota(jnp.int32, (cap, rows), 0).astype(jnp.float32)
    lane_id = lax.broadcasted_iota(jnp.int32, (cap, block_rows), 1).astype(jnp.float32)

    def pack(s, carry):
        sa, sb = s // nb, s % nb
        place = pos[pl.ds(s, 1), :]
        source = held[sa * 2 + sb % 2, sb // 2, pl.ds(0, rows), :]
        at = pl.multiple_of(s * cap, 16)
        for kind, block, out in ((0, b, st_ref), (1, 0, sth)):
            match = slot_id == rank[kind, pl.ds(s, 1), :]
            base = (block * block_rows).astype(jnp.float32) if kind == 0 else 0.0
            where = jnp.sum(jnp.where(match, place - base + 1.0, 0.0), axis=1, keepdims=True) - 1.0
            out[pl.ds(at, cap), :] = jnp.where(lane_id == where, 1.0, 0.0).astype(jnp.bfloat16)
            chosen = jnp.where(match, 1.0, 0.0).astype(jnp.bfloat16)
            packed[kind, pl.ds(at, cap), :] = jnp.dot(
                chosen, source, preferred_element_type=jnp.float32).astype(jnp.bfloat16)
        return carry

    lax.fori_loop(0, n_dev, pack, 0)
    piece = 256

    def unpack(i, carry):
        lanes = pl.ds(pl.multiple_of(i * piece, piece), piece)
        for kind, select, out in ((0, st_ref, x_ref), (1, sth, xh_ref)):
            out[lanes, :] = lax.dot_general(
                select[:, lanes], packed[kind], (((0,), (0,)), ((), ())),
                preferred_element_type=jnp.float32).astype(jnp.bfloat16)
        return carry

    lax.fori_loop(0, block_rows // piece, unpack, 0)

    def drain(k, carry):
        @pl.when((k <= bo) & (bo < lines - 1))
        def _():
            z_up(k).wait_send()

        @pl.when((k >= bo) & (bo > 0))
        def _():
            z_down(k).wait_send()

        x_send(k).wait_send()
        y_send(k).wait_send()
        dy_send(k).wait_send()
        dx_send(k).wait_send()
        for kind in range(4):
            core_send(kind, k).wait_send()
        return carry

    lax.fori_loop(0, lines, drain, 0)


def gather_blocks(features, positions, nb, cap, block_rows):
    rows, width = features.shape
    n_dev = 4 * nb
    lines = nb // 2
    digits = jnp.stack([positions // 256, positions % 256], axis=1).reshape(-1, rows)
    digits = jnp.pad(digits, ((0, 16 - digits.shape[0]), (0, width - rows))).astype(features.dtype)
    shard = jnp.concatenate([features, digits], axis=0)
    padded = rows + 16
    slots = n_dev * cap
    dma = pltpu.SemaphoreType.DMA
    vmem = pl.BlockSpec(memory_space=pltpu.VMEM)
    bf16 = jnp.bfloat16
    return pl.pallas_call(
        functools.partial(gather_kernel, (nb, rows, cap, block_rows)),
        out_shape=(
            jax.ShapeDtypeStruct((block_rows, width), bf16),
            jax.ShapeDtypeStruct((block_rows, width), bf16),
            jax.ShapeDtypeStruct((slots, block_rows), bf16),
        ),
        in_specs=[vmem],
        out_specs=(vmem, vmem, vmem),
        scratch_shapes=[
            pltpu.VMEM((8, lines, padded, width), bf16),
            pltpu.VMEM((n_dev, rows), jnp.float32),
            pltpu.VMEM((2, n_dev, rows), jnp.float32),
            pltpu.VMEM((2, slots, width), bf16),
            pltpu.VMEM((slots, block_rows), bf16),
            dma((2, lines)), dma((lines,)),
            dma((lines,)), dma((lines,)), dma((lines,)), dma((lines,)),
            dma((lines,)), dma((lines,)), dma((lines,)), dma((lines,)),
            dma((4, lines)), dma((4, lines)), dma(()),
        ],
        compiler_params=pltpu.CompilerParams(
            collective_id=0, has_side_effects=True, vmem_limit_bytes=60 * 2**20),
        name="gather_blocks",
    )(shard)


def masked_block(values, tiles):
    tile_count = tiles.shape[0]
    tile_edge = values.shape[0] // tile_count
    shaped = values.reshape(tile_count, tile_edge, tile_count, tile_edge)
    keep_mask = tiles.astype(values.dtype)[:, None, :, None]
    return (shaped * keep_mask).reshape(values.shape)


def body(
    features, positions, diag_values, column_values, row_values, tile_masks, up_weight, down_weight
):
    rows, width = features.shape
    arrow_count = positions.shape[0]
    nb = lax.axis_size("blk")
    n_dev = arrow_count * nb
    block_rows = diag_values.shape[0]
    capacity = rows // nb + max(rows // (2 * nb), 1)
    cap = (capacity + 15) // 16 * 16
    x, x_head, select = gather_blocks(features, positions, nb, cap, block_rows)
    dot = functools.partial(jnp.dot, preferred_element_type=jnp.float32)
    arm_term = dot(masked_block(row_values, tile_masks[2]), x).astype(jnp.bfloat16)
    local_sum = dot(masked_block(diag_values, tile_masks[0]), x)
    local_sum = local_sum + dot(masked_block(column_values, tile_masks[1]), x_head)
    is_head = lax.axis_index("blk") == 0
    arm_total = lax.psum(arm_term, "blk").astype(jnp.float32)
    results = jnp.where(is_head, local_sum + arm_total, local_sum).astype(jnp.bfloat16)
    picked = dot(select, results).astype(jnp.bfloat16)
    returned = lax.all_to_all(
        picked.reshape(n_dev, cap, width), ("arrow", "blk"), split_axis=0, concat_axis=0, tiled=True
    ).reshape(n_dev * cap, width)
    inside = (positions // block_rows)[:, None, :] == jnp.arange(nb, dtype=jnp.int32)[None, :, None]
    inside = inside.reshape(n_dev, rows)
    before = (jnp.arange(rows)[:, None] < jnp.arange(rows)[None, :]).astype(jnp.bfloat16)
    rank = jnp.where(inside, dot(inside.astype(jnp.bfloat16), before), -1.0).astype(jnp.int32)
    pick = (rank.T[:, :, None] == jnp.arange(cap, dtype=jnp.int32)[None, None, :]).astype(jnp.bfloat16)
    aggregate = dot(pick.reshape(rows, n_dev * cap), returned).astype(jnp.bfloat16)
    joined = jnp.concatenate([features, aggregate], axis=1)
    hidden = jax.nn.silu(dot(joined, up_weight)).astype(jnp.bfloat16)
    return dot(hidden, down_weight).astype(jnp.bfloat16)


def solution(mesh):
    in_specs = (
        P(("arrow", "blk"), None),
        P(None, ("arrow", "blk")),
        P("arrow", "blk"),
        P("arrow", "blk"),
        P("arrow", "blk"),
        P(None, "arrow", "blk"),
        P(),
        P(),
    )
    out_specs = P(("arrow", "blk"), None)
    return jax.shard_map(body, mesh=mesh, in_specs=in_specs, out_specs=out_specs, check_vma=False)
```

time: 269 us -> 219 us (0.81)
  the two profiles are of different devices: /device:TPU:21 before, /device:TPU:0 now
where the time goes in v1:
time: 219 us
  waiting for transfers between devices  113 us (52%)
  Pallas kernels  58.8 us (27%)
  matrix products  23.6 us (11%)
  between operations  13.5 us (6%)
  starting transfers between devices  4.19 us (2%)
  other arithmetic  3.25 us (1%)
  local copies, waits for them, and re-layouts  2.62 us (1%)
    psum x1, waiting for transfers between devices, body(): arm_total = lax.psum(arm_term, 'blk').astype(jnp.float32)  74.1 us
    pallas_call x1, Pallas kernels, gather_blocks(): pl.pallas_call(functools.partial(gather_kernel, (nb, rows, cap, block_row...  58.8 us
    all_to_all x1, waiting for transfers between devices, body(): lax.all_to_all(picked.reshape(n_dev, cap, width), ('arrow', 'blk'), split...  38.5 us
    dot_general x1, matrix products, body(): return dot(hidden, down_weight).astype(jnp.bfloat16)  8.96 us
    dot_general x1, matrix products, body(): picked = dot(select, results).astype(jnp.bfloat16)  7.69 us
  transfers between devices with their start and end apart: 2, of which 2 were waited for; matrix products, arithmetic and copies ran while one was open for 1% of the time, Pallas kernels for 0%

profile of v1, /device:TPU:0, one launch (start us, length us, event | category | flops | bytes accessed | tf_op | source)
XLA Modules:
  0.0 218.6 jit_solution(7754684880633937845)
XLA Ops:
  6.5 0.0 copy-start.1
  6.5 0.0 all-reduce.3.cloned.1.call-start
  6.5 0.9 add_select_fusion.3
  7.4 1.7 fusion.27.shard_ref
  9.1 58.8 %gather_blocks.1 = (bf16[1024,512]{1,0:T(8,128)(2,1)}, bf16[1024,512]{1,0:T(8,128)(2,1)}, bf16[1536,1024]{1,0:T(8,128)(2,1)}) custom-call(bf16[272,512]{1,0:T(8,128)(2,1)} %fusion.27.shard_ref), custom_call_target="tpu_custom_call" | custom-call | tf_op jit(solution)/shard_map/gather_blocks/pallas_call | solution.py:234
  67.9 0.7 convert.18
  68.6 0.3 mul.43
  69.0 0.0 copy-done.1
  69.0 3.6 %fusion.9 = bf16[1024,512]{1,0:T(8,128)(2,1)} fusion(bf16[1024,512]{1,0:T(8,128)(2,1)} %get-tuple-element.9, bf16[1024,1024]{1,0:T(8,128)(2,1)S(1)} %copy-done.1, bf16[128,8,8,128]{3,2,1,0:T(8,128)(2,1)S(1)} %bitcast.53), kind=kOutput, calls=%fused_computation.16 | convolution fusion | flops 1075314688 | bytes 6291456 | tf_op jit(solution)/shard_map/dot_general | solution.py:280
  72.6 0.0 copy-start.2
  72.6 0.0 copy-start.4
  72.6 0.0 all-reduce.3.cloned.1.call-update
  72.6 0.3 mul.40
  72.9 1.2 copy-done.2
  74.1 0.3 copy-done.4
  74.4 2.6 %fusion.3 = f32[1024,512]{1,0:T(8,128)} fusion(bf16[1024,512]{1,0:T(8,128)(2,1)S(1)} %copy-done.4, bf16[1024,1024]{1,0:T(8,128)(2,1)S(1)} %copy-done.2, bf16[128,8,8,128]{3,2,1,0:T(8,128)(2,1)S(1)} %bitcast.52), kind=kOutput, calls=%fused_computation.8 | convolution fusion | flops 1074790400 | bytes 7340032 | tf_op jit(solution)/shard_map/dot_general | solution.py:282
  77.0 0.0 copy-start.3
  77.0 74.1 %all-reduce.3.cloned.1.call-done = bf16[1024,512]{1,0:T(8,128)(2,1)} async-done(((bf16[1024,512]{1,0:T(8,128)(2,1)}), bf16[1024,512]{1,0:T(8,128)(2,1)}) %all-reduce.3.cloned.1.call-update) | async-done | bytes 1048592 | tf_op jit(solution)/shard_map/psum | solution.py:284
  151.1 0.3 mul.37
  151.5 0.0 copy-done.3
  151.5 7.7 %convolution_convert_fusion = bf16[1536,512]{1,0:T(8,128)(2,1)} fusion(bf16[1536,1024]{1,0:T(8,128)(2,1)} %get-tuple-element.8, bf16[1024,512]{1,0:T(8,128)(2,1)} %all-reduce.3.cloned.1.call-done, f32[1024,512]{1,0:T(8,128)} %fusion.3, bf16[1024,512]{1,0:T(8,128)(2,1)S(1)} %copy-done.3, bf16[1024,1024]{1,0:T(8,128)(2,1)} %param.10, ...), kind=kOutput, calls=%fused_computation.2 | convolution fusion | flops 2688811008 | bytes 13107201 | tf_op jit(solution)/shard_map/dot_general | solution.py:286
  159.2 4.2 %all-to-all-start = ((bf16[32,48,512]{2,1,0:T(8,128)(2,1)}), bf16[32,48,512]{2,1,0:T(8,128)(2,1)S(1)}, u32[]{:S(2)}, u32[]{:S(2)}) async-start(bf16[32,48,512]{2,1,0:T(8,128)(2,1)} %bitcast.54), calls=%async_computation | async-start | bytes 3145728 | tf_op jit(solution)/shard_map/all_to_all | solution.py:287
  163.4 0.1 eq.41
  163.4 0.2 fusion.14
  163.6 0.0 copy-start
  163.7 38.5 %all-to-all-done = bf16[32,48,512]{2,1,0:T(8,128)(2,1)S(1)} async-done(((bf16[32,48,512]{2,1,0:T(8,128)(2,1)}), bf16[32,48,512]{2,1,0:T(8,128)(2,1)S(1)}, u32[]{:S(2)}, u32[]{:S(2)}) %all-to-all-start) | async-done | bytes 1572896 | tf_op jit(solution)/shard_map/all_to_all | solution.py:287
  202.2 0.6 fusion.11
  202.8 0.0 copy-done
  202.8 9.0 %fusion.12 = bf16[256,512]{1,0:T(8,128)(2,1)} fusion(bf16[4096,512]{1,0:T(8,128)(2,1)} %param.15, bf16[1024,4096]{1,0:T(8,128)(2,1)} %param.14, bf16[256,512]{1,0:T(8,128)(2,1)S(1)} %fusion.11, bf16[256,512]{1,0:T(8,128)(2,1)S(1)} %copy-done), kind=kOutput, calls=%fused_computation.19 | convolution fusion | flops 3227648000 | bytes 13369344 | tf_op jit(solution)/shard_map/dot_general | solution.py:298
  (5 shorter events, 0.0 us)
Async XLA Ops:
  6.5 62.4 %copy-start.1 = (bf16[1024,1024]{1,0:T(8,128)(2,1)S(1)}, bf16[1024,1024]{1,0:T(8,128)(2,1)}, u32[]{:S(2)}) copy-start(bf16[1024,1024]{1,0:T(8,128)(2,1)} %param.12) | copy-start | bytes 6291460
  6.5 144.6 %all-reduce.3.cloned.1.call-start = ((), (), s32[]{:S(2)}) async-start(), calls=%async_computation.1 | async-start | bytes 2097152 | tf_op jit(solution)/shard_map/psum | solution.py:284
  72.6 1.6 copy-start.2
  72.6 1.9 copy-start.4
  77.0 74.5 %copy-start.3 = (bf16[1024,512]{1,0:T(8,128)(2,1)S(1)}, bf16[1024,512]{1,0:T(8,128)(2,1)}, u32[]{:S(2)}) copy-start(bf16[1024,512]{1,0:T(8,128)(2,1)} %get-tuple-element.9) | copy-start | bytes 3145732
  159.2 43.0 %all-to-all-start = ((bf16[32,48,512]{2,1,0:T(8,128)(2,1)}), bf16[32,48,512]{2,1,0:T(8,128)(2,1)S(1)}, u32[]{:S(2)}, u32[]{:S(2)}) async-start(bf16[32,48,512]{2,1,0:T(8,128)(2,1)} %bitcast.54), calls=%async_computation | async-start | bytes 3145728 | tf_op jit(solution)/shard_map/all_to_all | solution.py:287
  163.6 39.2 %copy-start = (bf16[256,512]{1,0:T(8,128)(2,1)S(1)}, bf16[256,512]{1,0:T(8,128)(2,1)}, u32[]{:S(2)}) copy-start(bf16[256,512]{1,0:T(8,128)(2,1)} %param.8) | copy-start | bytes 786436
Sparse Core Ops, SparseCore 0:
  72.7 78.3 all-reduce.2

commit v2 on v1

--- a/solution.py
+++ b/solution.py
@@ -10,8 +10,7 @@
 MESH = pl.DeviceIdType.MESH
 
 
-def gather_kernel(dims, shard_ref, x_ref, xh_ref, st_ref, held, pos, rank, packed, sth,
-                  zs, zr, xs, xr, ys, yr, dxs, dxr, dys, dyr, cs, cr, own_sem):
+def gather_kernel(dims, shard_ref, x_ref, xh_ref, st_ref, sth, held, pos, rank, packed, zs, zr, xs, xr, ys, yr, dxs, dxr, dys, dyr, cs, cr, own_sem):
     nb, rows, cap, block_rows = dims
     lines = nb // 2
     n_dev = 4 * nb
@@ -175,7 +174,7 @@
         sa, sb = s // nb, s % nb
         place = pos[pl.ds(s, 1), :]
         source = held[sa * 2 + sb % 2, sb // 2, pl.ds(0, rows), :]
-        at = pl.multiple_of(s * cap, 16)
+        at = pl.multiple_of((sb * 4 + sa) * cap, 16)
         for kind, block, out in ((0, b, st_ref), (1, 0, sth)):
             match = slot_id == rank[kind, pl.ds(s, 1), :]
             base = (block * block_rows).astype(jnp.float32) if kind == 0 else 0.0
@@ -237,15 +236,15 @@
             jax.ShapeDtypeStruct((block_rows, width), bf16),
             jax.ShapeDtypeStruct((block_rows, width), bf16),
             jax.ShapeDtypeStruct((slots, block_rows), bf16),
+            jax.ShapeDtypeStruct((slots, block_rows), bf16),
         ),
         in_specs=[vmem],
-        out_specs=(vmem, vmem, vmem),
+        out_specs=(vmem, vmem, vmem, vmem),
         scratch_shapes=[
             pltpu.VMEM((8, lines, padded, width), bf16),
             pltpu.VMEM((n_dev, rows), jnp.float32),
             pltpu.VMEM((2, n_dev, rows), jnp.float32),
             pltpu.VMEM((2, slots, width), bf16),
-            pltpu.VMEM((slots, block_rows), bf16),
             dma((2, lines)), dma((lines,)),
             dma((lines,)), dma((lines,)), dma((lines,)), dma((lines,)),
             dma((lines,)), dma((lines,)), dma((lines,)), dma((lines,)),
@@ -257,12 +256,253 @@
     )(shard)
 
 
-def masked_block(values, tiles):
-    tile_count = tiles.shape[0]
-    tile_edge = values.shape[0] // tile_count
-    shaped = values.reshape(tile_count, tile_edge, tile_count, tile_edge)
-    keep_mask = tiles.astype(values.dtype)[:, None, :, None]
-    return (shaped * keep_mask).reshape(values.shape)
+def return_kernel(dims, x_ref, xh_ref, st_ref, sth_ref, pick_ref, arm_pick_ref, mask_ref, diag_hbm,
+                  column_hbm, row_hbm, agg_ref, blocks, arm, results, slots_arm, beside_in, up_in,
+                  down_in, summed, total, arm_back, picked, returned, load_sem, ysend, yrecv, usend,
+                  urecv, dsend, drecv, asend, arecv, rsend, rrecv):
+    nb, cap = dims
+    lines = nb // 2
+    n_dev = 4 * nb
+    group = 4 * cap
+    block_rows, width = x_ref.shape
+    a, b = lax.axis_index("arrow"), lax.axis_index("blk")
+    bo, bi = b // 2, b % 2
+    me = b * 4 + a
+    beside, up, down = (a, bo * 2 + 1 - bi), (a, b + 2), (a, b - 2)
+    f32, bf16 = jnp.float32, jnp.bfloat16
+    tile = block_rows // mask_ref.shape[1]
+
+    loads = [pltpu.make_async_copy(ref, blocks.at[i], load_sem.at[i])
+             for i, ref in enumerate((row_hbm, diag_hbm, column_hbm))]
+    for load in loads:
+        load.start()
+
+    barrier = pltpu.get_barrier_semaphore()
+
+    def greet(s, carry):
+        @pl.when(s != me)
+        def _():
+            pl.semaphore_signal(barrier, inc=1, device_id=(s % 4, s // 4), device_id_type=MESH)
+        return carry
+
+    lax.fori_loop(0, n_dev, greet, 0)
+    pl.semaphore_wait(barrier, n_dev - 1)
+
+    def remote(src, dst, ssem, rsem, device):
+        return pltpu.make_async_remote_copy(src_ref=src, dst_ref=dst, send_sem=ssem, recv_sem=rsem,
+                                            device_id=device, device_id_type=MESH)
+
+    def y_copy(k):
+        return remote(slots_arm.at[k * 2 + 1 - bi], beside_in.at[k], ysend.at[k], yrecv.at[k], beside)
+
+    def up_copy(k):
+        return remote(summed.at[k], up_in.at[k], usend.at[k], urecv.at[k], up)
+
+    def down_copy(k):
+        return remote(summed.at[k], down_in.at[k], dsend.at[k], drecv.at[k], down)
+
+    def arm_copy(to, frm):
+        return remote(total.at[pl.ds(pl.multiple_of(to * cap, 16), cap)],
+                      arm_back.at[pl.ds(pl.multiple_of(frm * cap, 16), cap)],
+                      asend.at[to], arecv.at[frm], (to, b))
+
+    def back_copy(to, frm):
+        return remote(picked.at[to], returned.at[pl.ds(pl.multiple_of(frm * cap, 16), cap)],
+                      rsend.at[to], rrecv.at[frm], (to % 4, to // 4))
+
+    def masked(kind, i):
+        rows = pl.ds(pl.multiple_of(i * tile, tile), tile)
+        return blocks[kind, rows, :] * mask_ref[kind, pl.ds(i, 1), :].astype(bf16)
+
+    loads[0].wait()
+
+    def arm_tile(i, carry):
+        rows = pl.ds(pl.multiple_of(i * tile, tile), tile)
+        arm[rows, :] = jnp.dot(masked(0, i), x_ref[...], preferred_element_type=f32).astype(bf16)
+        return carry
+
+    lax.fori_loop(0, block_rows // tile, arm_tile, 0)
+
+    def place_arm(k):
+        rows = pl.ds(pl.multiple_of(k * group, 16), group)
+        slots_arm[k] = jnp.dot(sth_ref[rows, :], arm[...], preferred_element_type=f32).astype(bf16)
+
+    def far_first(d, body):
+        for sign in (-1, 1):
+            k = bo + sign * d
+            ok = (k >= 0) & (k < lines)
+            if sign == 1:
+                ok = ok & (d > 0)
+            pl.when(ok)(functools.partial(body, k))
+
+    def to_beside(i, carry):
+        def one(k):
+            place_arm(k * 2 + 1 - bi)
+            y_copy(k).start()
+        far_first(lines - 1 - i, one)
+        return carry
+
+    lax.fori_loop(0, lines, to_beside, 0)
+
+    def own_arm(k, carry):
+        place_arm(k * 2 + bi)
+        return carry
+
+    lax.fori_loop(0, lines, own_arm, 0)
+    loads[1].wait()
+    loads[2].wait()
+
+    def block_tile(i, carry):
+        rows = pl.ds(pl.multiple_of(i * tile, tile), tile)
+        results[rows, :] = (
+            jnp.dot(masked(1, i), x_ref[...], preferred_element_type=f32)
+            + jnp.dot(masked(2, i), xh_ref[...], preferred_element_type=f32)).astype(bf16)
+        return carry
+
+    lax.fori_loop(0, block_rows // tile, block_tile, 0)
+
+    def send_plane(k):
+        plane = 2 * group
+        rows = pl.ds(pl.multiple_of(k * plane, 16), plane)
+        found = jnp.dot(st_ref[rows, :], results[...], preferred_element_type=f32).astype(bf16)
+        picked[pl.ds(k * 8, 8)] = found.reshape(8, cap, width)
+
+        def one(i, carry):
+            to = k * 8 + i
+
+            @pl.when(to != me)
+            def _():
+                back_copy(to, me).start()
+            return carry
+
+        lax.fori_loop(0, 8, one, 0)
+
+    send_plane(bo)
+    returned[pl.ds(pl.multiple_of(me * cap, 16), cap), :] = picked[me]
+
+    def pair_sum(k):
+        y_copy(k).wait_recv()
+        return slots_arm[k * 2 + bi].astype(f32) + beside_in[k].astype(f32)
+
+    def outward(i, carry):
+        d = lines - 1 - i
+
+        def one(k):
+            summed[k] = pair_sum(k).astype(bf16)
+
+            @pl.when((k > bo) & (bo > 0))
+            def _():
+                up_copy(k).wait_recv()
+                summed[k] = (summed[k].astype(f32) + up_in[k].astype(f32)).astype(bf16)
+
+            @pl.when((k < bo) & (bo < lines - 1))
+            def _():
+                down_copy(k).wait_recv()
+                summed[k] = (summed[k].astype(f32) + down_in[k].astype(f32)).astype(bf16)
+
+            @pl.when(k > bo)
+            def _():
+                up_copy(k).start()
+
+            @pl.when(k < bo)
+            def _():
+                down_copy(k).start()
+
+            send_plane(k)
+
+        far_first(d, one)
+        return carry
+
+    lax.fori_loop(0, lines - 1, outward, 0)
+    total[...] = pair_sum(bo).astype(bf16)
+
+    @pl.when(bo > 0)
+    def _():
+        up_copy(bo).wait_recv()
+        total[...] = (total[...].astype(f32) + up_in[bo].astype(f32)).astype(bf16)
+
+    @pl.when(bo < lines - 1)
+    def _():
+        down_copy(bo).wait_recv()
+        total[...] = (total[...].astype(f32) + down_in[bo].astype(f32)).astype(bf16)
+
+    for to in range(4):
+        @pl.when(to != a)
+        def _():
+            arm_copy(to, a).start()
+
+    tail = arm_back.shape[0] - group
+    arm_back[pl.ds(group, tail), :] = jnp.zeros((tail, width), bf16)
+    own = pl.ds(pl.multiple_of(a * cap, 16), cap)
+    arm_back[own, :] = total[own, :]
+
+    def collect(s, carry):
+        @pl.when(s != me)
+        def _():
+            back_copy(me, s).wait_recv()
+            back_copy(s, me).wait_send()
+        return carry
+
+    lax.fori_loop(0, n_dev, collect, 0)
+    for frm in range(4):
+        @pl.when(frm != a)
+        def _():
+            arm_copy(a, frm).wait_recv()
+            arm_copy(frm, a).wait_send()
+
+    agg_ref[...] = (
+        jnp.dot(pick_ref[...], returned[...], preferred_element_type=f32)
+        + jnp.dot(arm_pick_ref[...], arm_back[...], preferred_element_type=f32)).astype(bf16)
+
+    def drain(k, carry):
+        y_copy(k).wait_send()
+
+        @pl.when(k > bo)
+        def _():
+            up_copy(k).wait_send()
+
+        @pl.when(k < bo)
+        def _():
+            down_copy(k).wait_send()
+        return carry
+
+    lax.fori_loop(0, lines, drain, 0)
+
+
+def return_rows(x, xh, select, select_head, pick, arm_pick, masks, diag, column, row, nb, cap):
+    block_rows, width = x.shape
+    n_dev = 4 * nb
+    lines = nb // 2
+    group = 4 * cap
+    dma = pltpu.SemaphoreType.DMA
+    vmem = pl.BlockSpec(memory_space=pltpu.VMEM)
+    hbm = pl.BlockSpec(memory_space=pl.ANY)
+    bf16 = jnp.bfloat16
+    return pl.pallas_call(
+        functools.partial(return_kernel, (nb, cap)),
+        out_shape=jax.ShapeDtypeStruct((pick.shape[0], width), bf16),
+        in_specs=[vmem] * 7 + [hbm] * 3,
+        out_specs=vmem,
+        scratch_shapes=[
+            pltpu.VMEM((3, block_rows, block_rows), bf16),
+            pltpu.VMEM((block_rows, width), bf16),
+            pltpu.VMEM((block_rows, width), bf16),
+            pltpu.VMEM((nb, group, width), bf16),
+            pltpu.VMEM((lines, group, width), bf16),
+            pltpu.VMEM((lines, group, width), bf16),
+            pltpu.VMEM((lines, group, width), bf16),
+            pltpu.VMEM((lines, group, width), bf16),
+            pltpu.VMEM((group, width), bf16),
+            pltpu.VMEM((arm_pick.shape[1], width), bf16),
+            pltpu.VMEM((n_dev, cap, width), bf16),
+            pltpu.VMEM((n_dev * cap, width), bf16),
+            dma((3,)), dma((lines,)), dma((lines,)), dma((lines,)), dma((lines,)),
+            dma((lines,)), dma((lines,)), dma((4,)), dma((4,)), dma((n_dev,)), dma((n_dev,)),
+        ],
+        compiler_params=pltpu.CompilerParams(
+            collective_id=1, has_side_effects=True, vmem_limit_bytes=56 * 2**20),
+        name="return_rows",
+    )(x, xh, select, select_head, pick, arm_pick, masks, diag, column, row)
 
 
 def body(
@@ -275,24 +515,20 @@
     block_rows = diag_values.shape[0]
     capacity = rows // nb + max(rows // (2 * nb), 1)
     cap = (capacity + 15) // 16 * 16
-    x, x_head, select = gather_blocks(features, positions, nb, cap, block_rows)
     dot = functools.partial(jnp.dot, preferred_element_type=jnp.float32)
-    arm_term = dot(masked_block(row_values, tile_masks[2]), x).astype(jnp.bfloat16)
-    local_sum = dot(masked_block(diag_values, tile_masks[0]), x)
-    local_sum = local_sum + dot(masked_block(column_values, tile_masks[1]), x_head)
-    is_head = lax.axis_index("blk") == 0
-    arm_total = lax.psum(arm_term, "blk").astype(jnp.float32)
-    results = jnp.where(is_head, local_sum + arm_total, local_sum).astype(jnp.bfloat16)
-    picked = dot(select, results).astype(jnp.bfloat16)
-    returned = lax.all_to_all(
-        picked.reshape(n_dev, cap, width), ("arrow", "blk"), split_axis=0, concat_axis=0, tiled=True
-    ).reshape(n_dev * cap, width)
-    inside = (positions // block_rows)[:, None, :] == jnp.arange(nb, dtype=jnp.int32)[None, :, None]
+    x, x_head, select, select_head = gather_blocks(features, positions, nb, cap, block_rows)
+    inside = (positions // block_rows)[None] == jnp.arange(nb, dtype=jnp.int32)[:, None, None]
     inside = inside.reshape(n_dev, rows)
     before = (jnp.arange(rows)[:, None] < jnp.arange(rows)[None, :]).astype(jnp.bfloat16)
     rank = jnp.where(inside, dot(inside.astype(jnp.bfloat16), before), -1.0).astype(jnp.int32)
     pick = (rank.T[:, :, None] == jnp.arange(cap, dtype=jnp.int32)[None, None, :]).astype(jnp.bfloat16)
-    aggregate = dot(pick.reshape(rows, n_dev * cap), returned).astype(jnp.bfloat16)
+    pick = pick.reshape(rows, n_dev * cap)
+    group = arrow_count * cap
+    arm_pick = jnp.pad(pick[:, :group], ((0, 0), (0, (group // 128 + 1) * 128 - group)))
+    masks = jnp.repeat(tile_masks, block_rows // tile_masks.shape[2], axis=2).astype(jnp.float32)
+    masks = jnp.stack([masks[2], masks[0], masks[1]])
+    aggregate = return_rows(x, x_head, select, select_head, pick, arm_pick, masks,
+                            diag_values, column_values, row_values, nb, cap)
     joined = jnp.concatenate([features, aggregate], axis=1)
     hidden = jax.nn.silu(dot(joined, up_weight)).astype(jnp.bfloat16)
     return dot(hidden, down_weight).astype(jnp.bfloat16)

time: 219 us -> 144 us (0.66)
  the two profiles are of different devices: /device:TPU:0 before, /device:TPU:21 now
where the time goes in v2:
time: 144 us; the launch traced here: 142 us
  Pallas kernels  127 us (88%)
  matrix products  9.07 us (6%)
  other arithmetic  4.66 us (3%)
    pallas_call x1, Pallas kernels, return_rows(): pl.pallas_call(functools.partial(return_kernel, (nb, cap)), out_shape=jax...  69.4 us
    pallas_call x1, Pallas kernels, gather_blocks(): pl.pallas_call(functools.partial(gather_kernel, (nb, rows, cap, block_row...  57.9 us
    dot_general x1, matrix products, body(): return dot(hidden, down_weight).astype(jnp.bfloat16)  8.88 us

profile of v2, /device:TPU:21, one launch (start us, length us, event | category | flops | bytes accessed | tf_op | source)
XLA Modules:
  0.0 142.3 jit_solution(10642099693083324437)
XLA Ops:
  0.0 0.0 copy-start.2
  0.0 0.1 eq.45
  0.1 0.7 add_select_fusion
  0.8 0.7 convert_element_type.25
  1.6 0.1 copy.16
  1.6 0.1 copy.15
  1.7 0.1 eq.51
  1.8 0.1 broadcast_bitcast_fusion.1
  1.9 0.2 fusion.3
  2.1 0.1 broadcast_bitcast_fusion
  2.2 0.7 pad_maximum_fusion.mask_ref
  2.8 1.7 %fusion.15.shard_ref = bf16[272,512]{1,0:T(8,128)(2,1)} fusion(bf16[8,256]{1,0:T(8,128)(2,1)S(1)} %reshape.17, bf16[256,512]{1,0:T(8,128)(2,1)} %param.8), kind=kLoop, calls=%fused_computation.13 | loop fusion | flops 835584 | bytes 544768 | tf_op jit(solution)/shard_map/concatenate | solution.py:227
  4.5 0.1 eq.48
  4.6 0.5 copy.14
  5.1 0.1 compare_convert_fusion.pick_ref
  5.3 0.0 copy-done.2
  5.3 0.0 copy-start
  5.3 0.7 slice_select_fusion.arm_pick_ref
  6.0 57.9 %gather_blocks.1 = (bf16[1024,512]{1,0:T(8,128)(2,1)}, bf16[1024,512]{1,0:T(8,128)(2,1)}, bf16[1536,1024]{1,0:T(8,128)(2,1)}, bf16[1536,1024]{1,0:T(8,128)(2,1)}) custom-call(bf16[272,512]{1,0:T(8,128)(2,1)} %fusion.15.shard_ref), custom_call_target="tpu_custom_call" | custom-call | tf_op jit(solution)/shard_map/gather_blocks/pallas_call | solution.py:233
  64.0 0.0 copy-done
  64.0 0.0 copy-start.1
  64.0 69.4 %return_rows.1 = bf16[256,512]{1,0:T(8,128)(2,1)} custom-call(bf16[1024,512]{1,0:T(8,128)(2,1)} %get-tuple-element.9.x_ref, bf16[1024,512]{1,0:T(8,128)(2,1)} %get-tuple-element.10.xh_ref, bf16[1536,1024]{1,0:T(8,128)(2,1)} %get-tuple-element.11.st_ref, bf16[1536,1024]{1,0:T(8,128)(2,1)} %get-tuple-element.12.sth_ref, bf16[256,1536]{1,0:T(8,128)(2,1)} %copy-done, ...), custom_call_target="tpu_custom_call" | custom-call | tf_op jit(solution)/shard_map/return_rows/pallas_call | solution.py:481
  133.4 0.0 copy-done.1
  133.4 8.9 %fusion.1 = bf16[256,512]{1,0:T(8,128)(2,1)} fusion(bf16[4096,512]{1,0:T(8,128)(2,1)} %param.15, bf16[1024,4096]{1,0:T(8,128)(2,1)} %param.14, bf16[256,512]{1,0:T(8,128)(2,1)} %return_rows.1, bf16[256,512]{1,0:T(8,128)(2,1)S(1)} %copy-done.1), kind=kOutput, calls=%fused_computation.3 | convolution fusion | flops 3227648000 | bytes 13369344 | tf_op jit(solution)/shard_map/dot_general | solution.py:534
  (9 shorter events, 0.1 us)
Async XLA Ops:
  0.0 5.3 %copy-start.2 = (pred[256]{0:T(512)(128)(4,1)S(1)}, pred[256]{0:T(512)(128)(4,1)}, u32[]{:S(2)}) copy-start(pred[256]{0:T(512)(128)(4,1)} %constant.48.clone.1) | copy-start | bytes 772
  5.3 58.7 %copy-start = (bf16[256,1536]{1,0:T(8,128)(2,1)}, bf16[256,1536]{1,0:T(8,128)(2,1)S(1)}, u32[]{:S(2)}) copy-start(bf16[256,1536]{1,0:T(8,128)(2,1)S(1)} %compare_convert_fusion.pick_ref) | copy-start | bytes 2359300
  64.0 69.4 %copy-start.1 = (bf16[256,512]{1,0:T(8,128)(2,1)S(1)}, bf16[256,512]{1,0:T(8,128)(2,1)}, u32[]{:S(2)}) copy-start(bf16[256,512]{1,0:T(8,128)(2,1)} %param.8) | copy-start | bytes 786436

commit v3 on v2

--- a/solution.py
+++ b/solution.py
@@ -10,11 +10,14 @@
 MESH = pl.DeviceIdType.MESH
 
 
-def gather_kernel(dims, shard_ref, x_ref, xh_ref, st_ref, sth, held, pos, rank, packed, zs, zr, xs, xr, ys, yr, dxs, dxr, dys, dyr, cs, cr, own_sem):
+def gather_kernel(dims, features_ref, positions_ref, x_ref, xh_ref, st_ref, sth_ref, rank_ref, held,
+                  digit_buf, packed, place_col, place_row, zs, zr, xs, xr, ys, yr, dxs, dxr, dys, dyr, cs, cr, own_sem):
     nb, rows, cap, block_rows = dims
     lines = nb // 2
     n_dev = 4 * nb
-    padded, width = shard_ref.shape
+    width = features_ref.shape[1]
+    padded = rows + 16
+    f32, bf16 = jnp.float32, jnp.bfloat16
     half = (padded // 2 + 15) // 16 * 16
     a, b = lax.axis_index("arrow"), lax.axis_index("blk")
     ao, c, bo, bi = a // 2, a % 2, b // 2, b % 2
@@ -63,8 +66,13 @@
     def core_send(kind, k):
         return send(cols[kind], k, whole_rows, cs.at[kind, k], cr.at[kind, k], core)
 
-    own = pltpu.make_async_copy(shard_ref, held.at[mine, bo], own_sem)
+    own = pltpu.make_async_copy(features_ref, held.at[mine, bo, pl.ds(0, rows)], own_sem)
     own.start()
+    place = positions_ref[...]
+    digit_buf[...] = jnp.zeros(digit_buf.shape, f32)
+    digit_buf[pl.ds(0, 4), pl.ds(0, rows)] = (place // 256).astype(f32)
+    digit_buf[pl.ds(4, 4), pl.ds(0, rows)] = (place % 256).astype(f32)
+    held[mine, bo, pl.ds(rows, 16), :] = digit_buf[...].astype(bf16)
     barrier = pltpu.get_barrier_semaphore()
     for device in (across, beside, core):
         pl.semaphore_signal(barrier, inc=1, device_id=device, device_id_type=MESH)
@@ -81,6 +89,39 @@
     pl.semaphore_wait(barrier, 3 + ends)
 
     own.wait()
+
+    q_row = lax.broadcasted_iota(jnp.int32, (16, 16), 0)
+    q_lane = lax.broadcasted_iota(jnp.int32, (16, 16), 1)
+    before = (lax.broadcasted_iota(jnp.int32, (rows, rows), 0)
+              < lax.broadcasted_iota(jnp.int32, (rows, rows), 1)).astype(f32).astype(bf16)
+
+    def ranks(digits, arrow, base):
+        weight = jnp.where(q_lane == arrow, 256.0, jnp.where(q_lane == arrow + 4, 1.0, 0.0)).astype(bf16)
+        place = jnp.dot(weight, digits, preferred_element_type=f32)
+        inside = (place >= base) & (place < base + block_rows)
+        count = jnp.dot(jnp.where(inside, 1.0, 0.0).astype(bf16), before, preferred_element_type=f32)
+        return place - base, jnp.where(inside, count, -1.0)
+
+    slot_id = lax.broadcasted_iota(jnp.int32, (cap, rows), 0).astype(f32)
+    lane_id = lax.broadcasted_iota(jnp.int32, (cap, block_rows), 1).astype(f32)
+    block_base = jnp.where(lax.broadcasted_iota(jnp.int32, (16, rows), 0) == 0,
+                           (b * block_rows).astype(f32), 0.0)
+
+    def pack(col, k):
+        at = pl.multiple_of(((k * 2 + col % 2) * 4 + col // 2) * cap, 16)
+        place, rank = ranks(held[col, k, pl.ds(rows, 16), pl.ds(0, rows)], a, block_base)
+        chosen = []
+        for kind, out in ((0, st_ref), (1, sth_ref)):
+            match = slot_id == rank[kind:kind + 1, :]
+            where = jnp.sum(jnp.where(match, place[kind:kind + 1, :] + 1.0, 0.0),
+                            axis=1, keepdims=True) - 1.0
+            out[pl.ds(at, cap), :] = jnp.where(lane_id == where, 1.0, 0.0).astype(bf16)
+            place_col[kind, pl.ds(at, cap), :] = jnp.broadcast_to(where, (cap, 128))
+            chosen.append(jnp.where(match, 1.0, 0.0).astype(bf16))
+        found = jnp.dot(jnp.concatenate(chosen, axis=0), held[col, k, pl.ds(0, rows), :],
+                        preferred_element_type=f32).astype(bf16)
+        packed[0, pl.ds(at, cap), :] = found[:cap]
+        packed[1, pl.ds(at, cap), :] = found[cap:]
 
     def step(t, carry):
         for sign in (-1, 1):
@@ -136,64 +177,53 @@
                 send(d_col, k3, low, dxs.at[k3], dxr.at[k3], across).wait_recv()
                 core_send(3, k3).start()
 
-        return carry
-
-    lax.fori_loop(0, lines + 2, step, 0)
-
-    def arrive(k, carry):
-        for kind in range(4):
-            send(other[kind], k, whole_rows, cs.at[kind, k], cr.at[kind, k], core).wait_recv()
-        return carry
-
-    lax.fori_loop(0, lines, arrive, 0)
-
-    extra = padded - rows
-    row_id = lax.broadcasted_iota(jnp.int32, (extra, rows), 0)
-    weight = jnp.where(row_id == 2 * a, 256.0, jnp.where(row_id == 2 * a + 1, 1.0, 0.0))
-
-    def read_pos(s, carry):
-        sa, sb = s // nb, s % nb
-        digits = held[sa * 2 + sb % 2, sb // 2, pl.ds(rows, extra), pl.ds(0, rows)]
-        pos[pl.ds(s, 1), :] = jnp.sum(digits.astype(jnp.float32) * weight, axis=0, keepdims=True)
-        return carry
-
-    lax.fori_loop(0, n_dev, read_pos, 0)
-    every = pos[...].astype(jnp.int32)
-    before = (lax.broadcasted_iota(jnp.int32, (rows, rows), 0)
-              < lax.broadcasted_iota(jnp.int32, (rows, rows), 1)).astype(jnp.float32).astype(jnp.bfloat16)
-    for kind, block in ((0, b), (1, 0)):
-        inside = (every >= block * block_rows) & (every < (block + 1) * block_rows)
-        count = jnp.dot(inside.astype(jnp.float32).astype(jnp.bfloat16), before,
-                        preferred_element_type=jnp.float32)
-        rank[kind] = jnp.where(inside, count, -1.0)
-
-    slot_id = lax.broadcasted_iota(jnp.int32, (cap, rows), 0).astype(jnp.float32)
-    lane_id = lax.broadcasted_iota(jnp.int32, (cap, block_rows), 1).astype(jnp.float32)
-
-    def pack(s, carry):
-        sa, sb = s // nb, s % nb
-        place = pos[pl.ds(s, 1), :]
-        source = held[sa * 2 + sb % 2, sb // 2, pl.ds(0, rows), :]
-        at = pl.multiple_of((sb * 4 + sa) * cap, 16)
-        for kind, block, out in ((0, b, st_ref), (1, 0, sth)):
-            match = slot_id == rank[kind, pl.ds(s, 1), :]
-            base = (block * block_rows).astype(jnp.float32) if kind == 0 else 0.0
-            where = jnp.sum(jnp.where(match, place - base + 1.0, 0.0), axis=1, keepdims=True) - 1.0
-            out[pl.ds(at, cap), :] = jnp.where(lane_id == where, 1.0, 0.0).astype(jnp.bfloat16)
-            chosen = jnp.where(match, 1.0, 0.0).astype(jnp.bfloat16)
-            packed[kind, pl.ds(at, cap), :] = jnp.dot(
-                chosen, source, preferred_element_type=jnp.float32).astype(jnp.bfloat16)
-        return carry
-
-    lax.fori_loop(0, n_dev, pack, 0)
+        def visit(i, inner):
+            sign, kind, far = i % 2 * 2 - 1, i // 2 % 4, i // 8
+            late = t - (kind + 1) // 2 - far
+            k = bo + sign * late
+            ok = (late >= 0) & (late < lines) & (k >= 0) & (k < lines) & ((late > 0) | (sign < 0))
+            col = column((ao + kind % 2) % 2, (c + far) % 2, (bi + kind // 2) % 2)
+
+            @pl.when(ok)
+            def _():
+                @pl.when(far == 1)
+                def _():
+                    send(col, k, whole_rows, cs.at[kind, k], cr.at[kind, k], core).wait_recv()
+
+                pack(col, k)
+            return inner
+
+        lax.fori_loop(0, 16, visit, 0)
+        return carry
+
+    lax.fori_loop(0, lines + 3, step, 0)
+
+    q = lax.broadcasted_iota(jnp.int32, (16, rows), 0)
+    plane_base = jnp.where(q < 8, (bo * 2 + q % 2) * block_rows, jnp.where(q < 12, 0, -block_rows)).astype(f32)
+    plane_arrow = jnp.where(q_row < 8, q_row // 2, q_row % 4)
+
+    def plane_ranks(k, carry):
+        rank_ref[k] = ranks(held[mine, k, pl.ds(rows, 16), pl.ds(0, rows)], plane_arrow, plane_base)[1]
+        return carry
+
+    lax.fori_loop(0, lines, plane_ranks, 0)
+
+    def turn(i, carry):
+        part = pl.ds(pl.multiple_of(i * 128, 128), 128)
+        for kind in range(2):
+            place_row[kind, :, part] = place_col[kind, part, :].T[0:8, :]
+        return carry
+
+    lax.fori_loop(0, place_row.shape[2] // 128, turn, 0)
     piece = 256
+    row_id = lax.broadcasted_iota(jnp.int32, (piece, place_row.shape[2]), 0).astype(f32)
 
     def unpack(i, carry):
-        lanes = pl.ds(pl.multiple_of(i * piece, piece), piece)
-        for kind, select, out in ((0, st_ref, x_ref), (1, sth, xh_ref)):
-            out[lanes, :] = lax.dot_general(
-                select[:, lanes], packed[kind], (((0,), (0,)), ((), ())),
-                preferred_element_type=jnp.float32).astype(jnp.bfloat16)
+        part = pl.ds(pl.multiple_of(i * piece, piece), piece)
+        for kind, out in ((0, x_ref), (1, xh_ref)):
+            target = place_row[kind, 0:1, :] - (i * piece).astype(f32)
+            select = jnp.where(row_id == target, 1.0, 0.0).astype(bf16)
+            out[part, :] = jnp.dot(select, packed[kind], preferred_element_type=f32).astype(bf16)
         return carry
 
     lax.fori_loop(0, block_rows // piece, unpack, 0)
@@ -222,9 +252,6 @@
     rows, width = features.shape
     n_dev = 4 * nb
     lines = nb // 2
-    digits = jnp.stack([positions // 256, positions % 256], axis=1).reshape(-1, rows)
-    digits = jnp.pad(digits, ((0, 16 - digits.shape[0]), (0, width - rows))).astype(features.dtype)
-    shard = jnp.concatenate([features, digits], axis=0)
     padded = rows + 16
     slots = n_dev * cap
     dma = pltpu.SemaphoreType.DMA
@@ -237,14 +264,16 @@
             jax.ShapeDtypeStruct((block_rows, width), bf16),
             jax.ShapeDtypeStruct((slots, block_rows), bf16),
             jax.ShapeDtypeStruct((slots, block_rows), bf16),
+            jax.ShapeDtypeStruct((lines, 16, rows), jnp.float32),
         ),
-        in_specs=[vmem],
-        out_specs=(vmem, vmem, vmem, vmem),
+        in_specs=[vmem, vmem],
+        out_specs=(vmem,) * 5,
         scratch_shapes=[
             pltpu.VMEM((8, lines, padded, width), bf16),
-            pltpu.VMEM((n_dev, rows), jnp.float32),
-            pltpu.VMEM((2, n_dev, rows), jnp.float32),
+            pltpu.VMEM((16, width), jnp.float32),
             pltpu.VMEM((2, slots, width), bf16),
+            pltpu.VMEM((2, slots, 128), jnp.float32),
+            pltpu.VMEM((2, 8, slots), jnp.float32),
             dma((2, lines)), dma((lines,)),
             dma((lines,)), dma((lines,)), dma((lines,)), dma((lines,)),
             dma((lines,)), dma((lines,)), dma((lines,)), dma((lines,)),
@@ -253,7 +282,7 @@
         compiler_params=pltpu.CompilerParams(
             collective_id=0, has_side_effects=True, vmem_limit_bytes=60 * 2**20),
         name="gather_blocks",
-    )(shard)
+    )(features, positions)
 
 
 def return_kernel(dims, x_ref, xh_ref, st_ref, sth_ref, pick_ref, arm_pick_ref, mask_ref, diag_hbm,
@@ -516,7 +545,7 @@
     capacity = rows // nb + max(rows // (2 * nb), 1)
     cap = (capacity + 15) // 16 * 16
     dot = functools.partial(jnp.dot, preferred_element_type=jnp.float32)
-    x, x_head, select, select_head = gather_blocks(features, positions, nb, cap, block_rows)
+    x, x_head, select, select_head, plane_rank = gather_blocks(features, positions, nb, cap, block_rows)
     inside = (positions // block_rows)[None] == jnp.arange(nb, dtype=jnp.int32)[:, None, None]
     inside = inside.reshape(n_dev, rows)
     before = (jnp.arange(rows)[:, None] < jnp.arange(rows)[None, :]).astype(jnp.bfloat16)

time: 144 us -> 142 us (0.986)
  other arithmetic: 4.66 us -> 2.93 us
    pallas_call x1, Pallas kernels: 57.9 us -> 56.1 us  [gather_blocks(): pl.pallas_call(functools.partial(gather_kernel, (nb, rows, cap, block_row...]
    concatenate x1 -> x0, other arithmetic: 1.7 us -> none  [gather_blocks(): shard = jnp.concatenate([features, digits], axis=0)]
    pallas_call x1, Pallas kernels: 69.4 us -> 70.9 us  [return_rows(): pl.pallas_call(functools.partial(return_kernel, (nb, cap)), out_shape=jax...]
where the time goes in v3:
time: 142 us; the launch traced here: 140 us
  Pallas kernels  127 us (89%)
  matrix products  9.14 us (6%)
  other arithmetic  2.93 us (2%)
    pallas_call x1, Pallas kernels, return_rows(): pl.pallas_call(functools.partial(return_kernel, (nb, cap)), out_shape=jax...  70.9 us
    pallas_call x1, Pallas kernels, gather_blocks(): pl.pallas_call(functools.partial(gather_kernel, (nb, rows, cap, block_row...  56.1 us
    dot_general x1, matrix products, body(): return dot(hidden, down_weight).astype(jnp.bfloat16)  8.95 us

profile of v3, /device:TPU:21, one launch (start us, length us, event | category | flops | bytes accessed | tf_op | source)
XLA Modules:
  0.0 140.2 jit_solution(4809323565822092887)
XLA Ops:
  0.0 0.0 copy-start.2
  0.0 0.7 add_select_fusion
  0.7 0.1 eq.43
  0.8 0.7 convert_element_type.24
  1.5 0.1 copy.14
  1.6 0.1 copy.13
  1.7 0.1 eq.49
  1.7 0.1 broadcast_bitcast_fusion.1
  1.8 0.2 fusion.3
  2.0 0.1 broadcast_bitcast_fusion
  2.1 0.7 pad_maximum_fusion.mask_ref
  2.8 0.1 eq.46
  2.9 0.5 copy.12
  3.4 0.1 compare_convert_fusion.pick_ref
  3.5 0.0 copy-done.2
  3.5 0.0 copy-start
  3.5 0.7 slice_select_fusion.arm_pick_ref
  4.2 56.1 %gather_blocks.1 = (bf16[1024,512]{1,0:T(8,128)(2,1)}, bf16[1024,512]{1,0:T(8,128)(2,1)}, bf16[1536,1024]{1,0:T(8,128)(2,1)}, bf16[1536,1024]{1,0:T(8,128)(2,1)}, f32[4,16,256]{2,1,0:T(8,128)}) custom-call(bf16[256,512]{1,0:T(8,128)(2,1)} %features_ref.1, s32[4,256]{1,0:T(4,128)} %positions_ref.1), custom_call_target="tpu_custom_call" | custom-call | tf_op jit(solution)/shard_map/gather_blocks/pallas_call | solution.py:260
  60.4 0.0 copy-done
  60.4 0.0 copy-start.1
  60.4 70.9 %return_rows.1 = bf16[256,512]{1,0:T(8,128)(2,1)} custom-call(bf16[1024,512]{1,0:T(8,128)(2,1)} %get-tuple-element.9.x_ref, bf16[1024,512]{1,0:T(8,128)(2,1)} %get-tuple-element.10.xh_ref, bf16[1536,1024]{1,0:T(8,128)(2,1)} %get-tuple-element.11.st_ref, bf16[1536,1024]{1,0:T(8,128)(2,1)} %get-tuple-element.12.sth_ref, bf16[256,1536]{1,0:T(8,128)(2,1)} %copy-done, ...), custom_call_target="tpu_custom_call" | custom-call | tf_op jit(solution)/shard_map/return_rows/pallas_call | solution.py:510
  131.3 0.0 copy-done.1
  131.3 8.9 %fusion.1 = bf16[256,512]{1,0:T(8,128)(2,1)} fusion(bf16[4096,512]{1,0:T(8,128)(2,1)} %param.15, bf16[1024,4096]{1,0:T(8,128)(2,1)} %param.14, bf16[256,512]{1,0:T(8,128)(2,1)} %return_rows.1, bf16[256,512]{1,0:T(8,128)(2,1)S(1)} %copy-done.1), kind=kOutput, calls=%fused_computation.3 | convolution fusion | flops 3227648000 | bytes 13369344 | tf_op jit(solution)/shard_map/dot_general | solution.py:563
  (6 shorter events, 0.0 us)
Async XLA Ops:
  0.0 3.5 %copy-start.2 = (pred[256]{0:T(512)(128)(4,1)S(1)}, pred[256]{0:T(512)(128)(4,1)}, u32[]{:S(2)}) copy-start(pred[256]{0:T(512)(128)(4,1)} %constant.23.clone.1) | copy-start | bytes 772
  3.5 56.9 %copy-start = (bf16[256,1536]{1,0:T(8,128)(2,1)}, bf16[256,1536]{1,0:T(8,128)(2,1)S(1)}, u32[]{:S(2)}) copy-start(bf16[256,1536]{1,0:T(8,128)(2,1)S(1)} %compare_convert_fusion.pick_ref) | copy-start | bytes 2359300
  60.4 70.9 %copy-start.1 = (bf16[256,512]{1,0:T(8,128)(2,1)S(1)}, bf16[256,512]{1,0:T(8,128)(2,1)}, u32[]{:S(2)}) copy-start(bf16[256,512]{1,0:T(8,128)(2,1)} %features_ref.1) | copy-start | bytes 786436

commit v4 on v3

--- a/solution.py
+++ b/solution.py
@@ -285,278 +285,187 @@
     )(features, positions)
 
 
-def return_kernel(dims, x_ref, xh_ref, st_ref, sth_ref, pick_ref, arm_pick_ref, mask_ref, diag_hbm,
-                  column_hbm, row_hbm, agg_ref, blocks, arm, results, slots_arm, beside_in, up_in,
-                  down_in, summed, total, arm_back, picked, returned, load_sem, ysend, yrecv, usend,
-                  urecv, dsend, drecv, asend, arecv, rsend, rrecv):
+def return_kernel(dims, x_ref, xh_ref, st_ref, sth_ref, rank_ref, tiles_ref, diag_hbm, column_hbm,
+                  row_hbm, agg_ref, blocks, masks, arm, results, outgoing, incoming, partial, column_in,
+                  load_sem, psend, precv, zsend, zrecv):
     nb, cap = dims
     lines = nb // 2
-    n_dev = 4 * nb
-    group = 4 * cap
     block_rows, width = x_ref.shape
     a, b = lax.axis_index("arrow"), lax.axis_index("blk")
     bo, bi = b // 2, b % 2
-    me = b * 4 + a
-    beside, up, down = (a, bo * 2 + 1 - bi), (a, b + 2), (a, b - 2)
+    me = bi * 4 + a
     f32, bf16 = jnp.float32, jnp.bfloat16
-    tile = block_rows // mask_ref.shape[1]
+    edge = tiles_ref.shape[1]
+    tile = block_rows // edge
 
     loads = [pltpu.make_async_copy(ref, blocks.at[i], load_sem.at[i])
-             for i, ref in enumerate((row_hbm, diag_hbm, column_hbm))]
+             for i, ref in enumerate((diag_hbm, column_hbm, row_hbm))]
     for load in loads:
         load.start()
 
     barrier = pltpu.get_barrier_semaphore()
 
-    def greet(s, carry):
-        @pl.when(s != me)
-        def _():
-            pl.semaphore_signal(barrier, inc=1, device_id=(s % 4, s // 4), device_id_type=MESH)
-        return carry
-
-    lax.fori_loop(0, n_dev, greet, 0)
-    pl.semaphore_wait(barrier, n_dev - 1)
-
-    def remote(src, dst, ssem, rsem, device):
-        return pltpu.make_async_remote_copy(src_ref=src, dst_ref=dst, send_sem=ssem, recv_sem=rsem,
-                                            device_id=device, device_id_type=MESH)
-
-    def y_copy(k):
-        return remote(slots_arm.at[k * 2 + 1 - bi], beside_in.at[k], ysend.at[k], yrecv.at[k], beside)
-
-    def up_copy(k):
-        return remote(summed.at[k], up_in.at[k], usend.at[k], urecv.at[k], up)
-
-    def down_copy(k):
-        return remote(summed.at[k], down_in.at[k], dsend.at[k], drecv.at[k], down)
-
-    def arm_copy(to, frm):
-        return remote(total.at[pl.ds(pl.multiple_of(to * cap, 16), cap)],
-                      arm_back.at[pl.ds(pl.multiple_of(frm * cap, 16), cap)],
-                      asend.at[to], arecv.at[frm], (to, b))
-
-    def back_copy(to, frm):
-        return remote(picked.at[to], returned.at[pl.ds(pl.multiple_of(frm * cap, 16), cap)],
-                      rsend.at[to], rrecv.at[frm], (to % 4, to // 4))
+    def greet(to, carry):
+        @pl.when(to != me)
+        def _():
+            pl.semaphore_signal(barrier, inc=1, device_id=(to % 4, bo * 2 + to // 4),
+                                device_id_type=MESH)
+        return carry
+
+    def greet_column(k, carry):
+        @pl.when(k != bo)
+        def _():
+            pl.semaphore_signal(barrier, inc=1, device_id=(a, k * 2 + bi), device_id_type=MESH)
+        return carry
+
+    lax.fori_loop(0, 8, greet, 0)
+    lax.fori_loop(0, lines, greet_column, 0)
+    spread = (lax.broadcasted_iota(jnp.int32, (edge, block_rows), 1) // tile
+              == lax.broadcasted_iota(jnp.int32, (edge, block_rows), 0)).astype(f32)
+    for kind in range(3):
+        masks[kind] = jnp.dot(tiles_ref[kind].astype(f32), spread, preferred_element_type=f32)
 
     def masked(kind, i):
         rows = pl.ds(pl.multiple_of(i * tile, tile), tile)
-        return blocks[kind, rows, :] * mask_ref[kind, pl.ds(i, 1), :].astype(bf16)
-
-    loads[0].wait()
-
-    def arm_tile(i, carry):
-        rows = pl.ds(pl.multiple_of(i * tile, tile), tile)
-        arm[rows, :] = jnp.dot(masked(0, i), x_ref[...], preferred_element_type=f32).astype(bf16)
-        return carry
-
-    lax.fori_loop(0, block_rows // tile, arm_tile, 0)
-
-    def place_arm(k):
-        rows = pl.ds(pl.multiple_of(k * group, 16), group)
-        slots_arm[k] = jnp.dot(sth_ref[rows, :], arm[...], preferred_element_type=f32).astype(bf16)
-
-    def far_first(d, body):
-        for sign in (-1, 1):
-            k = bo + sign * d
-            ok = (k >= 0) & (k < lines)
-            if sign == 1:
-                ok = ok & (d > 0)
-            pl.when(ok)(functools.partial(body, k))
-
-    def to_beside(i, carry):
-        def one(k):
-            place_arm(k * 2 + 1 - bi)
-            y_copy(k).start()
-        far_first(lines - 1 - i, one)
-        return carry
-
-    lax.fori_loop(0, lines, to_beside, 0)
-
-    def own_arm(k, carry):
-        place_arm(k * 2 + bi)
-        return carry
-
-    lax.fori_loop(0, lines, own_arm, 0)
-    loads[1].wait()
-    loads[2].wait()
+        return blocks[kind, rows, :] * masks[kind, pl.ds(i, 1), :].astype(bf16)
+
+    for load in loads:
+        load.wait()
 
     def block_tile(i, carry):
         rows = pl.ds(pl.multiple_of(i * tile, tile), tile)
+        arm[rows, :] = jnp.dot(masked(2, i), x_ref[...], preferred_element_type=f32).astype(bf16)
         results[rows, :] = (
-            jnp.dot(masked(1, i), x_ref[...], preferred_element_type=f32)
-            + jnp.dot(masked(2, i), xh_ref[...], preferred_element_type=f32)).astype(bf16)
-        return carry
-
-    lax.fori_loop(0, block_rows // tile, block_tile, 0)
-
-    def send_plane(k):
-        plane = 2 * group
-        rows = pl.ds(pl.multiple_of(k * plane, 16), plane)
-        found = jnp.dot(st_ref[rows, :], results[...], preferred_element_type=f32).astype(bf16)
-        picked[pl.ds(k * 8, 8)] = found.reshape(8, cap, width)
-
-        def one(i, carry):
-            to = k * 8 + i
-
+            jnp.dot(masked(0, i), x_ref[...], preferred_element_type=f32)
+            + jnp.dot(masked(1, i), xh_ref[...], preferred_element_type=f32)).astype(bf16)
+        return carry
+
+    lax.fori_loop(0, edge, block_tile, 0)
+    pl.semaphore_wait(barrier, 7 + lines - 1)
+
+    def plane_copy(k, to, frm):
+        return pltpu.make_async_remote_copy(
+            src_ref=outgoing.at[k, to], dst_ref=incoming.at[k, frm], send_sem=psend.at[k, to],
+            recv_sem=precv.at[k, frm], device_id=(to % 4, bo * 2 + to // 4), device_id_type=MESH)
+
+    def column_copy(to, frm):
+        return pltpu.make_async_remote_copy(
+            src_ref=partial.at[to], dst_ref=column_in.at[frm], send_sem=zsend.at[to],
+            recv_sem=zrecv.at[frm], device_id=(a, to * 2 + bi), device_id_type=MESH)
+
+    def far_first(body):
+        def step(i, carry):
+            late = lines - 1 - i // 2
+            k = bo + (i % 2 * 2 - 1) * late
+            pl.when((k >= 0) & (k < lines) & ((late > 0) | (i % 2 == 0)))(functools.partial(body, k))
+            return carry
+        lax.fori_loop(0, 2 * lines, step, 0)
+
+    def send_chunk(k):
+        chunk = 8 * cap
+        rows = pl.ds(pl.multiple_of(k * chunk, 16), chunk)
+        for kind, select, values in ((0, st_ref, results), (1, sth_ref, arm)):
+            found = jnp.dot(select[rows, :], values[...], preferred_element_type=f32).astype(bf16)
+            outgoing[k, :, pl.ds(kind * cap, cap), :] = found.reshape(8, cap, width)
+
+        def one(to, carry):
             @pl.when(to != me)
             def _():
-                back_copy(to, me).start()
+                plane_copy(k, to, me).start()
             return carry
 
         lax.fori_loop(0, 8, one, 0)
-
-    send_plane(bo)
-    returned[pl.ds(pl.multiple_of(me * cap, 16), cap), :] = picked[me]
-
-    def pair_sum(k):
-        y_copy(k).wait_recv()
-        return slots_arm[k * 2 + bi].astype(f32) + beside_in[k].astype(f32)
-
-    def outward(i, carry):
-        d = lines - 1 - i
-
-        def one(k):
-            summed[k] = pair_sum(k).astype(bf16)
-
-            @pl.when((k > bo) & (bo > 0))
-            def _():
-                up_copy(k).wait_recv()
-                summed[k] = (summed[k].astype(f32) + up_in[k].astype(f32)).astype(bf16)
-
-            @pl.when((k < bo) & (bo < lines - 1))
-            def _():
-                down_copy(k).wait_recv()
-                summed[k] = (summed[k].astype(f32) + down_in[k].astype(f32)).astype(bf16)
-
-            @pl.when(k > bo)
-            def _():
-                up_copy(k).start()
-
-            @pl.when(k < bo)
-            def _():
-                down_copy(k).start()
-
-            send_plane(k)
-
-        far_first(d, one)
-        return carry
-
-    lax.fori_loop(0, lines - 1, outward, 0)
-    total[...] = pair_sum(bo).astype(bf16)
-
-    @pl.when(bo > 0)
-    def _():
-        up_copy(bo).wait_recv()
-        total[...] = (total[...].astype(f32) + up_in[bo].astype(f32)).astype(bf16)
-
-    @pl.when(bo < lines - 1)
-    def _():
-        down_copy(bo).wait_recv()
-        total[...] = (total[...].astype(f32) + down_in[bo].astype(f32)).astype(bf16)
-
-    for to in range(4):
-        @pl.when(to != a)
-        def _():
-            arm_copy(to, a).start()
-
-    tail = arm_back.shape[0] - group
-    arm_back[pl.ds(group, tail), :] = jnp.zeros((tail, width), bf16)
-    own = pl.ds(pl.multiple_of(a * cap, 16), cap)
-    arm_back[own, :] = total[own, :]
-
-    def collect(s, carry):
-        @pl.when(s != me)
-        def _():
-            back_copy(me, s).wait_recv()
-            back_copy(s, me).wait_send()
-        return carry
-
-    lax.fori_loop(0, n_dev, collect, 0)
-    for frm in range(4):
-        @pl.when(frm != a)
-        def _():
-            arm_copy(a, frm).wait_recv()
-            arm_copy(frm, a).wait_send()
-
-    agg_ref[...] = (
-        jnp.dot(pick_ref[...], returned[...], preferred_element_type=f32)
-        + jnp.dot(arm_pick_ref[...], arm_back[...], preferred_element_type=f32)).astype(bf16)
+        incoming[k, me] = outgoing[k, me]
+
+    far_first(send_chunk)
+    lane = lax.broadcasted_iota(jnp.int32, (16, 16 * cap), 1)
+    frm = lane // (2 * cap)
+    source = jnp.where(lane // cap % 2 == 0, frm % 4 * 2 + frm // 4, 8 + frm % 4)
+    expand = (lax.broadcasted_iota(jnp.int32, (16, 16 * cap), 0) == source).astype(f32).astype(bf16)
+    slot = (lax.broadcasted_iota(jnp.int32, (1, 16 * cap), 1) % cap).astype(f32)
+
+    def sum_chunk(k):
+        held = lax.dot_general(rank_ref[k].astype(bf16), expand, (((0,), (0,)), ((), ())),
+                               preferred_element_type=f32)
+        gather = jnp.where(held == slot, 1.0, 0.0).astype(bf16)
+
+        def one(frm, carry):
+            @pl.when(frm != me)
+            def _():
+                plane_copy(k, me, frm).wait_recv()
+            return carry
+
+        lax.fori_loop(0, 8, one, 0)
+        partial[k] = jnp.dot(gather, incoming[k].reshape(16 * cap, width),
+                             preferred_element_type=f32).astype(bf16)
+
+        @pl.when(k != bo)
+        def _():
+            column_copy(k, bo).start()
+
+    far_first(sum_chunk)
 
     def drain(k, carry):
-        y_copy(k).wait_send()
-
-        @pl.when(k > bo)
-        def _():
-            up_copy(k).wait_send()
-
-        @pl.when(k < bo)
-        def _():
-            down_copy(k).wait_send()
+        def one(to, inner):
+            @pl.when(to != me)
+            def _():
+                plane_copy(k, to, me).wait_send()
+            return inner
+
+        lax.fori_loop(0, 8, one, 0)
+
+        @pl.when(k != bo)
+        def _():
+            column_copy(k, bo).wait_send()
+            column_copy(bo, k).wait_recv()
         return carry
 
     lax.fori_loop(0, lines, drain, 0)
-
-
-def return_rows(x, xh, select, select_head, pick, arm_pick, masks, diag, column, row, nb, cap):
+    column_in[bo] = partial[bo]
+    agg_ref[...] = jnp.sum(column_in[...].astype(f32), axis=0).astype(bf16)
+
+
+def return_rows(x, xh, select, select_head, plane_rank, tiles, diag, column, row, nb, cap):
     block_rows, width = x.shape
-    n_dev = 4 * nb
-    lines = nb // 2
-    group = 4 * cap
+    lines, _, rows = plane_rank.shape
     dma = pltpu.SemaphoreType.DMA
     vmem = pl.BlockSpec(memory_space=pltpu.VMEM)
     hbm = pl.BlockSpec(memory_space=pl.ANY)
     bf16 = jnp.bfloat16
     return pl.pallas_call(
         functools.partial(return_kernel, (nb, cap)),
-        out_shape=jax.ShapeDtypeStruct((pick.shape[0], width), bf16),
-        in_specs=[vmem] * 7 + [hbm] * 3,
+        out_shape=jax.ShapeDtypeStruct((rows, width), bf16),
+        in_specs=[vmem] * 6 + [hbm] * 3,
         out_specs=vmem,
         scratch_shapes=[
             pltpu.VMEM((3, block_rows, block_rows), bf16),
+            pltpu.VMEM((3, tiles.shape[1], block_rows), jnp.float32),
             pltpu.VMEM((block_rows, width), bf16),
             pltpu.VMEM((block_rows, width), bf16),
-            pltpu.VMEM((nb, group, width), bf16),
-            pltpu.VMEM((lines, group, width), bf16),
-            pltpu.VMEM((lines, group, width), bf16),
-            pltpu.VMEM((lines, group, width), bf16),
-            pltpu.VMEM((lines, group, width), bf16),
-            pltpu.VMEM((group, width), bf16),
-            pltpu.VMEM((arm_pick.shape[1], width), bf16),
-            pltpu.VMEM((n_dev, cap, width), bf16),
-            pltpu.VMEM((n_dev * cap, width), bf16),
-            dma((3,)), dma((lines,)), dma((lines,)), dma((lines,)), dma((lines,)),
-            dma((lines,)), dma((lines,)), dma((4,)), dma((4,)), dma((n_dev,)), dma((n_dev,)),
+            pltpu.VMEM((lines, 8, 2 * cap, width), bf16),
+            pltpu.VMEM((lines, 8, 2 * cap, width), bf16),
+            pltpu.VMEM((lines, rows, width), bf16),
+            pltpu.VMEM((lines, rows, width), bf16),
+            dma((3,)), dma((lines, 8)), dma((lines, 8)), dma((lines,)), dma((lines,)),
         ],
         compiler_params=pltpu.CompilerParams(
             collective_id=1, has_side_effects=True, vmem_limit_bytes=56 * 2**20),
         name="return_rows",
-    )(x, xh, select, select_head, pick, arm_pick, masks, diag, column, row)
+    )(x, xh, select, select_head, plane_rank, tiles, diag, column, row)
 
 
 def body(
     features, positions, diag_values, column_values, row_values, tile_masks, up_weight, down_weight
 ):
-    rows, width = features.shape
-    arrow_count = positions.shape[0]
+    rows = features.shape[0]
     nb = lax.axis_size("blk")
-    n_dev = arrow_count * nb
     block_rows = diag_values.shape[0]
     capacity = rows // nb + max(rows // (2 * nb), 1)
     cap = (capacity + 15) // 16 * 16
     dot = functools.partial(jnp.dot, preferred_element_type=jnp.float32)
-    x, x_head, select, select_head, plane_rank = gather_blocks(features, positions, nb, cap, block_rows)
-    inside = (positions // block_rows)[None] == jnp.arange(nb, dtype=jnp.int32)[:, None, None]
-    inside = inside.reshape(n_dev, rows)
-    before = (jnp.arange(rows)[:, None] < jnp.arange(rows)[None, :]).astype(jnp.bfloat16)
-    rank = jnp.where(inside, dot(inside.astype(jnp.bfloat16), before), -1.0).astype(jnp.int32)
-    pick = (rank.T[:, :, None] == jnp.arange(cap, dtype=jnp.int32)[None, None, :]).astype(jnp.bfloat16)
-    pick = pick.reshape(rows, n_dev * cap)
-    group = arrow_count * cap
-    arm_pick = jnp.pad(pick[:, :group], ((0, 0), (0, (group // 128 + 1) * 128 - group)))
-    masks = jnp.repeat(tile_masks, block_rows // tile_masks.shape[2], axis=2).astype(jnp.float32)
-    masks = jnp.stack([masks[2], masks[0], masks[1]])
-    aggregate = return_rows(x, x_head, select, select_head, pick, arm_pick, masks,
+    x, x_head, select, select_head, plane_rank = gather_blocks(
+        features, positions, nb, cap, block_rows)
+    aggregate = return_rows(x, x_head, select, select_head, plane_rank, tile_masks,
                             diag_values, column_values, row_values, nb, cap)
     joined = jnp.concatenate([features, aggregate], axis=1)
     hidden = jax.nn.silu(dot(joined, up_weight)).astype(jnp.bfloat16)

time: 142 us -> 117 us (0.82)
  Pallas kernels: 127 us -> 107 us
  other arithmetic: 2.93 us -> 0 us
    pallas_call x1, Pallas kernels: 70.9 us -> 51.4 us  [return_rows(): pl.pallas_call(functools.partial(return_kernel, (nb, cap)), out_shape=jax...]
where the time goes in v4:
time: 117 us; the launch traced here: 116 us
  Pallas kernels  107 us (91%)
  matrix products  8.88 us (8%)
    pallas_call x1, Pallas kernels, gather_blocks(): pl.pallas_call(functools.partial(gather_kernel, (nb, rows, cap, block_row...  56.1 us
    pallas_call x1, Pallas kernels, return_rows(): pl.pallas_call(functools.partial(return_kernel, (nb, cap)), out_shape=jax...  51.4 us
    dot_general x1, matrix products, body(): return dot(hidden, down_weight).astype(jnp.bfloat16)  8.88 us

profile of v4, /device:TPU:21, one launch (start us, length us, event | category | flops | bytes accessed | tf_op | source)
XLA Modules:
  0.0 116.4 jit_solution(13893717080422729403)
XLA Ops:
  0.0 56.1 %gather_blocks.1 = (bf16[1024,512]{1,0:T(8,128)(2,1)}, bf16[1024,512]{1,0:T(8,128)(2,1)}, bf16[1536,1024]{1,0:T(8,128)(2,1)}, bf16[1536,1024]{1,0:T(8,128)(2,1)}, f32[4,16,256]{2,1,0:T(8,128)}) custom-call(bf16[256,512]{1,0:T(8,128)(2,1)} %features_ref.1, s32[4,256]{1,0:T(4,128)} %positions_ref.1), custom_call_target="tpu_custom_call" | custom-call | tf_op jit(solution)/shard_map/gather_blocks/pallas_call | solution.py:260
  56.1 0.0 copy-start
  56.1 51.4 %return_rows.1 = bf16[256,512]{1,0:T(8,128)(2,1)} custom-call(bf16[1024,512]{1,0:T(8,128)(2,1)} %get-tuple-element.10.x_ref, bf16[1024,512]{1,0:T(8,128)(2,1)} %get-tuple-element.11.xh_ref, bf16[1536,1024]{1,0:T(8,128)(2,1)} %get-tuple-element.12.st_ref, bf16[1536,1024]{1,0:T(8,128)(2,1)} %get-tuple-element.13.sth_ref, ...), custom_call_target="tpu_custom_call" | custom-call | tf_op jit(solution)/shard_map/return_rows/pallas_call | solution.py:435
  107.5 0.0 copy-done
  107.5 8.9 %fusion.1 = bf16[256,512]{1,0:T(8,128)(2,1)} fusion(bf16[4096,512]{1,0:T(8,128)(2,1)} %param.15, bf16[1024,4096]{1,0:T(8,128)(2,1)} %param.14, bf16[256,512]{1,0:T(8,128)(2,1)} %return_rows.1, bf16[256,512]{1,0:T(8,128)(2,1)S(1)} %copy-done), kind=kOutput, calls=%fused_computation.2 | convolution fusion | flops 3227648000 | bytes 13369344 | tf_op jit(solution)/shard_map/dot_general | solution.py:472
Async XLA Ops:
  56.1 51.4 %copy-start = (bf16[256,512]{1,0:T(8,128)(2,1)S(1)}, bf16[256,512]{1,0:T(8,128)(2,1)}, u32[]{:S(2)}) copy-start(bf16[256,512]{1,0:T(8,128)(2,1)} %features_ref.1) | copy-start | bytes 786436

commit v5 on v4

--- a/solution.py
+++ b/solution.py
@@ -11,7 +11,7 @@
 
 
 def gather_kernel(dims, features_ref, positions_ref, x_ref, xh_ref, st_ref, sth_ref, rank_ref, held,
-                  digit_buf, packed, place_col, place_row, zs, zr, xs, xr, ys, yr, dxs, dxr, dys, dyr, cs, cr, own_sem):
+                  digit_buf, packed, sums, place_col, place_row, zs, zr, xs, xr, ys, yr, dxs, dxr, dys, dyr, cs, cr, own_sem):
     nb, rows, cap, block_rows = dims
     lines = nb // 2
     n_dev = 4 * nb
@@ -85,6 +85,7 @@
     def _():
         pl.semaphore_signal(barrier, inc=1, device_id=down, device_id_type=MESH)
 
+    sums[...] = jnp.zeros(sums.shape, f32)
     ends = (bo < lines - 1).astype(jnp.int32) + (bo > 0).astype(jnp.int32)
     pl.semaphore_wait(barrier, 3 + ends)
 
@@ -123,6 +124,28 @@
         packed[0, pl.ds(at, cap), :] = found[:cap]
         packed[1, pl.ds(at, cap), :] = found[cap:]
 
+    chunk = 8 * cap
+    piece = 256
+    row_id = lax.broadcasted_iota(jnp.int32, (piece, chunk), 0).astype(f32)
+
+    def unpack(k):
+        start = k * chunk
+        for kind in range(2):
+            for i in range(chunk // 128):
+                part = pl.ds(pl.multiple_of(start + i * 128, 128), 128)
+                place_row[kind, :, pl.ds(i * 128, 128)] = place_col[kind, part, :].T[0:8, :]
+
+        def one(i, carry):
+            part = pl.ds(pl.multiple_of(i * piece, piece), piece)
+            slots = pl.ds(pl.multiple_of(start, 128), chunk)
+            for kind in range(2):
+                target = place_row[kind, 0:1, :] - (i * piece).astype(f32)
+                select = jnp.where(row_id == target, 1.0, 0.0).astype(bf16)
+                sums[kind, part, :] += jnp.dot(select, packed[kind, slots, :], preferred_element_type=f32)
+            return carry
+
+        lax.fori_loop(0, block_rows // piece, one, 0)
+
     def step(t, carry):
         for sign in (-1, 1):
             k = bo + sign * t
@@ -194,6 +217,15 @@
             return inner
 
         lax.fori_loop(0, 16, visit, 0)
+
+        def finish(i, inner):
+            late = t - 3
+            k = bo + (i * 2 - 1) * late
+            ok = (late >= 0) & (k >= 0) & (k < lines) & ((late > 0) | (i == 0))
+            pl.when(ok)(functools.partial(unpack, k))
+            return inner
+
+        lax.fori_loop(0, 2, finish, 0)
         return carry
 
     lax.fori_loop(0, lines + 3, step, 0)
@@ -208,25 +240,8 @@
 
     lax.fori_loop(0, lines, plane_ranks, 0)
 
-    def turn(i, carry):
-        part = pl.ds(pl.multiple_of(i * 128, 128), 128)
-        for kind in range(2):
-            place_row[kind, :, part] = place_col[kind, part, :].T[0:8, :]
-        return carry
-
-    lax.fori_loop(0, place_row.shape[2] // 128, turn, 0)
-    piece = 256
-    row_id = lax.broadcasted_iota(jnp.int32, (piece, place_row.shape[2]), 0).astype(f32)
-
-    def unpack(i, carry):
-        part = pl.ds(pl.multiple_of(i * piece, piece), piece)
-        for kind, out in ((0, x_ref), (1, xh_ref)):
-            target = place_row[kind, 0:1, :] - (i * piece).astype(f32)
-            select = jnp.where(row_id == target, 1.0, 0.0).astype(bf16)
-            out[part, :] = jnp.dot(select, packed[kind], preferred_element_type=f32).astype(bf16)
-        return carry
-
-    lax.fori_loop(0, block_rows // piece, unpack, 0)
+    x_ref[...] = sums[0].astype(bf16)
+    xh_ref[...] = sums[1].astype(bf16)
 
     def drain(k, carry):
         @pl.when((k <= bo) & (bo < lines - 1))
@@ -272,8 +287,9 @@
             pltpu.VMEM((8, lines, padded, width), bf16),
             pltpu.VMEM((16, width), jnp.float32),
             pltpu.VMEM((2, slots, width), bf16),
+            pltpu.VMEM((2, block_rows, width), jnp.float32),
             pltpu.VMEM((2, slots, 128), jnp.float32),
-            pltpu.VMEM((2, 8, slots), jnp.float32),
+            pltpu.VMEM((2, 8, 8 * cap), jnp.float32),
             dma((2, lines)), dma((lines,)),
             dma((lines,)), dma((lines,)), dma((lines,)), dma((lines,)),
             dma((lines,)), dma((lines,)), dma((lines,)), dma((lines,)),
@@ -285,9 +301,9 @@
     )(features, positions)
 
 
-def return_kernel(dims, x_ref, xh_ref, st_ref, sth_ref, rank_ref, tiles_ref, diag_hbm, column_hbm,
-                  row_hbm, agg_ref, blocks, masks, arm, results, outgoing, incoming, partial, column_in,
-                  load_sem, psend, precv, zsend, zrecv):
+def return_kernel(dims, x_ref, xh_ref, st_ref, sth_ref, rank_ref, tiles_ref, features_ref, diag_hbm,
+                  column_hbm, row_hbm, up_hbm, down_hbm, out_ref, blocks, up_weight, down_weight, early,
+                  acc, masks, arm, results, outgoing, incoming, partial, column_in, load_sem, psend, precv, zsend, zrecv):
     nb, cap = dims
     lines = nb // 2
     block_rows, width = x_ref.shape
@@ -300,6 +316,8 @@
 
     loads = [pltpu.make_async_copy(ref, blocks.at[i], load_sem.at[i])
              for i, ref in enumerate((diag_hbm, column_hbm, row_hbm))]
+    loads.append(pltpu.make_async_copy(up_hbm, up_weight, load_sem.at[3]))
+    loads.append(pltpu.make_async_copy(down_hbm, down_weight, load_sem.at[4]))
     for load in loads:
         load.start()
 
@@ -329,7 +347,7 @@
         rows = pl.ds(pl.multiple_of(i * tile, tile), tile)
         return blocks[kind, rows, :] * masks[kind, pl.ds(i, 1), :].astype(bf16)
 
-    for load in loads:
+    for load in loads[:3]:
         load.wait()
 
     def block_tile(i, carry):
@@ -378,6 +396,18 @@
         incoming[k, me] = outgoing[k, me]
 
     far_first(send_chunk)
+    loads[3].wait()
+    hidden_width = up_weight.shape[1]
+    part = 512
+
+    def first_half(i, carry):
+        lanes = pl.ds(pl.multiple_of(i * part, part), part)
+        early[:, lanes] = jnp.dot(features_ref[...], up_weight[pl.ds(0, width), lanes],
+                                  preferred_element_type=f32)
+        return carry
+
+    lax.fori_loop(0, hidden_width // part, first_half, 0)
+    loads[4].wait()
     lane = lax.broadcasted_iota(jnp.int32, (16, 16 * cap), 1)
     frm = lane // (2 * cap)
     source = jnp.where(lane // cap % 2 == 0, frm % 4 * 2 + frm // 4, 8 + frm % 4)
@@ -422,10 +452,24 @@
 
     lax.fori_loop(0, lines, drain, 0)
     column_in[bo] = partial[bo]
-    agg_ref[...] = jnp.sum(column_in[...].astype(f32), axis=0).astype(bf16)
-
-
-def return_rows(x, xh, select, select_head, plane_rank, tiles, diag, column, row, nb, cap):
+    aggregate = jnp.sum(column_in[...].astype(f32), axis=0).astype(bf16)
+    partial[0] = aggregate
+    acc[...] = jnp.zeros(acc.shape, f32)
+
+    def mlp(i, carry):
+        lanes = pl.ds(pl.multiple_of(i * part, part), part)
+        value = early[:, lanes] + jnp.dot(partial[0], up_weight[pl.ds(width, width), lanes],
+                                          preferred_element_type=f32)
+        hidden = (value / (1.0 + jnp.exp(-value))).astype(bf16)
+        acc[...] += jnp.dot(hidden, down_weight[lanes, :], preferred_element_type=f32)
+        return carry
+
+    lax.fori_loop(0, hidden_width // part, mlp, 0)
+    out_ref[...] = acc[...].astype(bf16)
+
+
+def return_rows(x, xh, select, select_head, plane_rank, tiles, features, diag, column, row, up, down,
+                nb, cap):
     block_rows, width = x.shape
     lines, _, rows = plane_rank.shape
     dma = pltpu.SemaphoreType.DMA
@@ -435,10 +479,14 @@
     return pl.pallas_call(
         functools.partial(return_kernel, (nb, cap)),
         out_shape=jax.ShapeDtypeStruct((rows, width), bf16),
-        in_specs=[vmem] * 6 + [hbm] * 3,
+        in_specs=[vmem] * 7 + [hbm] * 5,
         out_specs=vmem,
         scratch_shapes=[
             pltpu.VMEM((3, block_rows, block_rows), bf16),
+            pltpu.VMEM(up.shape, bf16),
+            pltpu.VMEM(down.shape, bf16),
+            pltpu.VMEM((rows, up.shape[1]), jnp.float32),
+            pltpu.VMEM((rows, width), jnp.float32),
             pltpu.VMEM((3, tiles.shape[1], block_rows), jnp.float32),
             pltpu.VMEM((block_rows, width), bf16),
             pltpu.VMEM((block_rows, width), bf16),
@@ -446,12 +494,12 @@
             pltpu.VMEM((lines, 8, 2 * cap, width), bf16),
             pltpu.VMEM((lines, rows, width), bf16),
             pltpu.VMEM((lines, rows, width), bf16),
-            dma((3,)), dma((lines, 8)), dma((lines, 8)), dma((lines,)), dma((lines,)),
+            dma((5,)), dma((lines, 8)), dma((lines, 8)), dma((lines,)), dma((lines,)),
         ],
         compiler_params=pltpu.CompilerParams(
-            collective_id=1, has_side_effects=True, vmem_limit_bytes=56 * 2**20),
+            collective_id=1, has_side_effects=True, vmem_limit_bytes=60 * 2**20),
         name="return_rows",
-    )(x, xh, select, select_head, plane_rank, tiles, diag, column, row)
+    )(x, xh, select, select_head, plane_rank, tiles, features, diag, column, row, up, down)
 
 
 def body(
@@ -462,14 +510,10 @@
     block_rows = diag_values.shape[0]
     capacity = rows // nb + max(rows // (2 * nb), 1)
     cap = (capacity + 15) // 16 * 16
-    dot = functools.partial(jnp.dot, preferred_element_type=jnp.float32)
     x, x_head, select, select_head, plane_rank = gather_blocks(
         features, positions, nb, cap, block_rows)
-    aggregate = return_rows(x, x_head, select, select_head, plane_rank, tile_masks,
-                            diag_values, column_values, row_values, nb, cap)
-    joined = jnp.concatenate([features, aggregate], axis=1)
-    hidden = jax.nn.silu(dot(joined, up_weight)).astype(jnp.bfloat16)
-    return dot(hidden, down_weight).astype(jnp.bfloat16)
+    return return_rows(x, x_head, select, select_head, plane_rank, tile_masks, features,
+                       diag_values, column_values, row_values, up_weight, down_weight, nb, cap)
 
 
 def solution(mesh):

time: 117 us -> 117 us (level)
  matrix products: 8.88 us -> 0 us
  Pallas kernels: 107 us -> 115 us
  local copies, waits for them, and re-layouts: 0.01 us -> 1.67 us
    dot_general x1 -> x0, matrix products: 8.88 us -> none  [body(): return dot(hidden, down_weight).astype(jnp.bfloat16)]
    pallas_call x1, Pallas kernels: 51.4 us -> 57.2 us  [return_rows(): pl.pallas_call(functools.partial(return_kernel, (nb, cap)), out_shape=jax...]
    pallas_call x1, Pallas kernels: 56.1 us -> 57.8 us  [gather_blocks(): pl.pallas_call(functools.partial(gather_kernel, (nb, rows, cap, block_row...]
    unnamed x2 -> x1, local copies, waits for them, and re-layouts: 0.01 us -> 1.67 us
where the time goes in v5:
time: 117 us
  Pallas kernels  115 us (98%)
  local copies, waits for them, and re-layouts  1.67 us (1%)
    pallas_call x1, Pallas kernels, gather_blocks(): pl.pallas_call(functools.partial(gather_kernel, (nb, rows, cap, block_row...  57.8 us
    pallas_call x1, Pallas kernels, return_rows(): pl.pallas_call(functools.partial(return_kernel, (nb, cap)), out_shape=jax...  57.2 us

profile of v5, /device:TPU:21, one launch (start us, length us, event | category | flops | bytes accessed | tf_op | source)
XLA Modules:
  0.0 116.7 jit_solution(14789638430225230275)
XLA Ops:
  0.0 57.8 %gather_blocks.1 = (bf16[1024,512]{1,0:T(8,128)(2,1)}, bf16[1024,512]{1,0:T(8,128)(2,1)}, bf16[1536,1024]{1,0:T(8,128)(2,1)}, bf16[1536,1024]{1,0:T(8,128)(2,1)}, f32[4,16,256]{2,1,0:T(8,128)}) custom-call(bf16[256,512]{1,0:T(8,128)(2,1)} %features_ref.3, s32[4,256]{1,0:T(4,128)} %positions_ref.1), custom_call_target="tpu_custom_call" | custom-call | tf_op jit(solution)/shard_map/gather_blocks/pallas_call | solution.py:275
  57.8 57.2 %return_rows.1 = bf16[256,512]{1,0:T(8,128)(2,1)} custom-call(bf16[1024,512]{1,0:T(8,128)(2,1)} %get-tuple-element.10.x_ref, bf16[1024,512]{1,0:T(8,128)(2,1)} %get-tuple-element.11.xh_ref, bf16[1536,1024]{1,0:T(8,128)(2,1)} %get-tuple-element.12.st_ref, bf16[1536,1024]{1,0:T(8,128)(2,1)} %get-tuple-element.13.sth_ref, ...), custom_call_target="tpu_custom_call" | custom-call | tf_op jit(solution)/shard_map/return_rows/pallas_call | solution.py:479
  115.0 1.7 %copy.10 = bf16[256,512]{1,0:T(8,128)(2,1)} copy(bf16[256,512]{1,0:T(8,128)(2,1)} %return_rows.1) | data formatting | bytes 524288

commit v6 on v5

--- a/solution.py
+++ b/solution.py
@@ -11,7 +11,7 @@
 
 
 def gather_kernel(dims, features_ref, positions_ref, x_ref, xh_ref, st_ref, sth_ref, rank_ref, held,
-                  digit_buf, packed, sums, place_col, place_row, zs, zr, xs, xr, ys, yr, dxs, dxr, dys, dyr, cs, cr, own_sem):
+                  digit_buf, packed, place_col, place_row, zs, zr, xs, xr, ys, yr, dxs, dxr, dys, dyr, cs, cr, own_sem):
     nb, rows, cap, block_rows = dims
     lines = nb // 2
     n_dev = 4 * nb
@@ -85,7 +85,6 @@
     def _():
         pl.semaphore_signal(barrier, inc=1, device_id=down, device_id_type=MESH)
 
-    sums[...] = jnp.zeros(sums.shape, f32)
     ends = (bo < lines - 1).astype(jnp.int32) + (bo > 0).astype(jnp.int32)
     pl.semaphore_wait(barrier, 3 + ends)
 
@@ -124,29 +123,23 @@
         packed[0, pl.ds(at, cap), :] = found[:cap]
         packed[1, pl.ds(at, cap), :] = found[cap:]
 
-    chunk = 8 * cap
-    piece = 256
-    row_id = lax.broadcasted_iota(jnp.int32, (piece, chunk), 0).astype(f32)
-
-    def unpack(k):
-        start = k * chunk
-        for kind in range(2):
-            for i in range(chunk // 128):
-                part = pl.ds(pl.multiple_of(start + i * 128, 128), 128)
-                place_row[kind, :, pl.ds(i * 128, 128)] = place_col[kind, part, :].T[0:8, :]
-
-        def one(i, carry):
-            part = pl.ds(pl.multiple_of(i * piece, piece), piece)
-            slots = pl.ds(pl.multiple_of(start, 128), chunk)
-            for kind in range(2):
-                target = place_row[kind, 0:1, :] - (i * piece).astype(f32)
-                select = jnp.where(row_id == target, 1.0, 0.0).astype(bf16)
-                sums[kind, part, :] += jnp.dot(select, packed[kind, slots, :], preferred_element_type=f32)
-            return carry
-
-        lax.fori_loop(0, block_rows // piece, one, 0)
-
     def step(t, carry):
+        def visit(i, inner):
+            sign, kind, far = i % 2 * 2 - 1, i // 2 % 4, i // 8
+            late = t - 1 - (kind + 1) // 2 - far
+            k = bo + sign * late
+            ok = (late >= 0) & (late < lines) & (k >= 0) & (k < lines) & ((late > 0) | (sign < 0))
+            col = column((ao + kind % 2) % 2, (c + far) % 2, (bi + kind // 2) % 2)
+
+            @pl.when(ok)
+            def _():
+                @pl.when(far == 1)
+                def _():
+                    send(col, k, whole_rows, cs.at[kind, k], cr.at[kind, k], core).wait_recv()
+
+                pack(col, k)
+            return inner
+
         for sign in (-1, 1):
             k = bo + sign * t
             ok = (k >= 0) & (k < lines) & (t < lines)
@@ -171,6 +164,7 @@
                 y_send(k).start()
                 core_send(0, k).start()
 
+        lax.fori_loop(0, 6, visit, 0)
         for sign in (-1, 1):
             t2 = t - 1
             k2 = bo + sign * t2
@@ -187,6 +181,7 @@
                 dx_send(k2).start()
                 core_send(2, k2).start()
 
+        lax.fori_loop(6, 11, visit, 0)
         for sign in (-1, 1):
             t3 = t - 2
             k3 = bo + sign * t3
@@ -200,35 +195,10 @@
                 send(d_col, k3, low, dxs.at[k3], dxr.at[k3], across).wait_recv()
                 core_send(3, k3).start()
 
-        def visit(i, inner):
-            sign, kind, far = i % 2 * 2 - 1, i // 2 % 4, i // 8
-            late = t - (kind + 1) // 2 - far
-            k = bo + sign * late
-            ok = (late >= 0) & (late < lines) & (k >= 0) & (k < lines) & ((late > 0) | (sign < 0))
-            col = column((ao + kind % 2) % 2, (c + far) % 2, (bi + kind // 2) % 2)
-
-            @pl.when(ok)
-            def _():
-                @pl.when(far == 1)
-                def _():
-                    send(col, k, whole_rows, cs.at[kind, k], cr.at[kind, k], core).wait_recv()
-
-                pack(col, k)
-            return inner
-
-        lax.fori_loop(0, 16, visit, 0)
-
-        def finish(i, inner):
-            late = t - 3
-            k = bo + (i * 2 - 1) * late
-            ok = (late >= 0) & (k >= 0) & (k < lines) & ((late > 0) | (i == 0))
-            pl.when(ok)(functools.partial(unpack, k))
-            return inner
-
-        lax.fori_loop(0, 2, finish, 0)
-        return carry
-
-    lax.fori_loop(0, lines + 3, step, 0)
+        lax.fori_loop(11, 16, visit, 0)
+        return carry
+
+    lax.fori_loop(0, lines + 4, step, 0)
 
     q = lax.broadcasted_iota(jnp.int32, (16, rows), 0)
     plane_base = jnp.where(q < 8, (bo * 2 + q % 2) * block_rows, jnp.where(q < 12, 0, -block_rows)).astype(f32)
@@ -240,8 +210,25 @@
 
     lax.fori_loop(0, lines, plane_ranks, 0)
 
-    x_ref[...] = sums[0].astype(bf16)
-    xh_ref[...] = sums[1].astype(bf16)
+    def turn(i, carry):
+        part = pl.ds(pl.multiple_of(i * 128, 128), 128)
+        for kind in range(2):
+            place_row[kind, :, part] = place_col[kind, part, :].T[0:8, :]
+        return carry
+
+    lax.fori_loop(0, place_row.shape[2] // 128, turn, 0)
+    piece = 256
+    row_id = lax.broadcasted_iota(jnp.int32, (piece, place_row.shape[2]), 0).astype(f32)
+
+    def unpack(i, carry):
+        part = pl.ds(pl.multiple_of(i * piece, piece), piece)
+        for kind, out in ((0, x_ref), (1, xh_ref)):
+            target = place_row[kind, 0:1, :] - (i * piece).astype(f32)
+            select = jnp.where(row_id == target, 1.0, 0.0).astype(bf16)
+            out[part, :] = jnp.dot(select, packed[kind], preferred_element_type=f32).astype(bf16)
+        return carry
+
+    lax.fori_loop(0, block_rows // piece, unpack, 0)
 
     def drain(k, carry):
         @pl.when((k <= bo) & (bo < lines - 1))
@@ -287,9 +274,8 @@
             pltpu.VMEM((8, lines, padded, width), bf16),
             pltpu.VMEM((16, width), jnp.float32),
             pltpu.VMEM((2, slots, width), bf16),
-            pltpu.VMEM((2, block_rows, width), jnp.float32),
             pltpu.VMEM((2, slots, 128), jnp.float32),
-            pltpu.VMEM((2, 8, 8 * cap), jnp.float32),
+            pltpu.VMEM((2, 8, slots), jnp.float32),
             dma((2, lines)), dma((lines,)),
             dma((lines,)), dma((lines,)), dma((lines,)), dma((lines,)),
             dma((lines,)), dma((lines,)), dma((lines,)), dma((lines,)),

time: 117 us -> 115 us (0.983)
  Pallas kernels: 115 us -> 113 us
    pallas_call x1, Pallas kernels: 57.8 us -> 55.6 us  [gather_blocks(): pl.pallas_call(functools.partial(gather_kernel, (nb, rows, cap, block_row...]
where the time goes in v6:
time: 115 us
  Pallas kernels  113 us (98%)
  local copies, waits for them, and re-layouts  1.67 us (1%)
    pallas_call x1, Pallas kernels, return_rows(): pl.pallas_call(functools.partial(return_kernel, (nb, cap)), out_shape=jax...  57.2 us
    pallas_call x1, Pallas kernels, gather_blocks(): pl.pallas_call(functools.partial(gather_kernel, (nb, rows, cap, block_row...  55.6 us

profile of v6, /device:TPU:21, one launch (start us, length us, event | category | flops | bytes accessed | tf_op | source)
XLA Modules:
  0.0 114.5 jit_solution(5193685790033812286)
XLA Ops:
  0.0 55.6 %gather_blocks.1 = (bf16[1024,512]{1,0:T(8,128)(2,1)}, bf16[1024,512]{1,0:T(8,128)(2,1)}, bf16[1536,1024]{1,0:T(8,128)(2,1)}, bf16[1536,1024]{1,0:T(8,128)(2,1)}, f32[4,16,256]{2,1,0:T(8,128)}) custom-call(bf16[256,512]{1,0:T(8,128)(2,1)} %features_ref.3, s32[4,256]{1,0:T(4,128)} %positions_ref.1), custom_call_target="tpu_custom_call" | custom-call | tf_op jit(solution)/shard_map/gather_blocks/pallas_call | solution.py:262
  55.6 57.2 %return_rows.1 = bf16[256,512]{1,0:T(8,128)(2,1)} custom-call(bf16[1024,512]{1,0:T(8,128)(2,1)} %get-tuple-element.10.x_ref, bf16[1024,512]{1,0:T(8,128)(2,1)} %get-tuple-element.11.xh_ref, bf16[1536,1024]{1,0:T(8,128)(2,1)} %get-tuple-element.12.st_ref, bf16[1536,1024]{1,0:T(8,128)(2,1)} %get-tuple-element.13.sth_ref, ...), custom_call_target="tpu_custom_call" | custom-call | tf_op jit(solution)/shard_map/return_rows/pallas_call | solution.py:465
  112.9 1.7 %copy.10 = bf16[256,512]{1,0:T(8,128)(2,1)} copy(bf16[256,512]{1,0:T(8,128)(2,1)} %return_rows.1) | data formatting | bytes 524288
